TPU v7x, 32 devices: a whole 2x2x4 slice. The times are simulated.
32 devices in a mesh: sp: 4 (over x, core), fsdp: 8 (over z, y).
Axes of the slice: x: 2, y: 2, z: 4, core: 2. Of those that a mesh axis runs over, the one named last changes fastest.
Arguments:
- tokens: bfloat16 [8, 1536, 768], P('fsdp', 'sp'), may hold values from -6 to 6
- w_query: bfloat16 [768, 768], P('fsdp'), may hold values from -0.21875 to 0.21875
- w_key: bfloat16 [768, 768], P('fsdp'), may hold values from -0.21875 to 0.21875
- w_value: bfloat16 [768, 768], P('fsdp'), may hold values from -0.21875 to 0.21875
- w_out: bfloat16 [768, 768], P('fsdp'), may hold values from -1.75 to 1.75
- gain_one: bfloat16 [768], P('fsdp'), may hold values from 0.5 to 1.5
- shift_one: bfloat16 [768], P('fsdp'), may hold values from -1 to 1
- w_gate: bfloat16 [768, 3072], P('fsdp'), may hold values from -0.21875 to 0.21875
- w_up: bfloat16 [768, 3072], P('fsdp'), may hold values from -0.21875 to 0.21875
- w_down: bfloat16 [3072, 768], P('fsdp'), may hold values from -0.21875 to 0.21875
- gain_two: bfloat16 [768], P('fsdp'), may hold values from 0.5 to 1.5
- shift_two: bfloat16 [768], P('fsdp'), may hold values from -1 to 1
- slopes: float32 [12], replicated, may hold values from 0.00390625 to 0.7071
- cotangent: bfloat16 [8, 1536, 768], P('fsdp', 'sp'), may hold values from -6 to 6
Outputs:
- output: bfloat16 [8, 1536, 768], P('fsdp', 'sp')
- input_grad: bfloat16 [8, 1536, 768], P('fsdp', 'sp')
- grad_query: float32 [768, 768], P('fsdp')
- grad_key: float32 [768, 768], P('fsdp')
- grad_value: float32 [768, 768], P('fsdp')
- grad_out: float32 [768, 768], P('fsdp')
- grad_gain_one: float32 [768], P('fsdp')
- grad_shift_one: float32 [768], P('fsdp')
- grad_gate: float32 [768, 3072], P('fsdp')
- grad_up: float32 [768, 3072], P('fsdp')
- grad_down: float32 [3072, 768], P('fsdp')
- grad_gain_two: float32 [768], P('fsdp')
- grad_shift_two: float32 [768], P('fsdp')
All inputs are finite; a program needn't handle non-finite values.
Results may differ from a plain program's by a relative error of at most 0.018.
Values may be sent and summed in bfloat16 or wider, within the bound.
A program may use at most 192 MiB of HBM per device.

v0:
```python
import jax
import jax.numpy as jnp
from jax import lax
from jax.sharding import PartitionSpec as P

HEADS = 12
HEAD_DIM = 64
GROUP = 4


EPS = 1e-12


def from_partner(array, axis, distance):
    return lax.ppermute(array, axis, [(i, i ^ 1 << distance) for i in range(lax.axis_size(axis))])


def normalize(residual_sum, gain, shift):
    average = jnp.mean(residual_sum, axis=-1, keepdims=True)
    centred = residual_sum - average
    spread = jnp.mean(centred * centred, axis=-1, keepdims=True)
    return centred * lax.rsqrt(spread + EPS) * gain + shift


def geglu(gate, upward):
    return jax.nn.gelu(gate, approximate=False) * upward


def product(left, right):
    return jnp.dot(left, right, preferred_element_type=jnp.float32)


def product_left(left, right):
    return lax.dot_general(
        left, right, (((0,), (0,)), ((), ())), preferred_element_type=jnp.float32
    )


def product_right(left, right):
    return lax.dot_general(
        left, right, (((1,), (1,)), ((), ())), preferred_element_type=jnp.float32
    )


def scores_of(block_queries, head_keys, slope, start):
    raw = product_right(block_queries, head_keys)
    places = start + jnp.arange(block_queries.shape[0], dtype=jnp.float32)
    columns = jnp.arange(head_keys.shape[0], dtype=jnp.float32)
    return raw * 0.125 - slope * jnp.abs(places[:, None] - columns[None, :])


def attend_forward(queries, keys, values, slopes, offset, block):
    heads, count, width = queries.shape
    number = count // block
    blocks = queries.reshape(heads, number, block, width)
    starts = offset + block * jnp.arange(number, dtype=jnp.float32)

    def per_head(items):
        head_queries, head_keys, head_values, slope = items

        def per_block(pair):
            block_queries, start = pair
            scores = scores_of(block_queries, head_keys, slope, start)
            highest = jnp.max(scores, axis=-1, keepdims=True)
            raised = jnp.exp(scores - highest)
            totals = jnp.sum(raised, axis=-1, keepdims=True)
            weights = (raised / totals).astype(jnp.bfloat16)
            context = product(weights, head_values)
            return (context, (highest + jnp.log(totals))[:, 0])

        return lax.map(per_block, (head_queries, starts))

    context, logsum = lax.map(per_head, (blocks, keys, values, slopes))
    return (context.reshape(heads, count, width), logsum.reshape(heads, count))


def attend_backward(queries, keys, values, d_context, logsum, slopes, offset, block):
    heads, count, width = queries.shape
    number = count // block
    query_blocks = queries.reshape(heads, number, block, width)
    grad_blocks = d_context.reshape(heads, number, block, width)
    logsum_blocks = logsum.reshape(heads, number, block)
    starts = offset + block * jnp.arange(number, dtype=jnp.float32)

    def per_head(items):
        head_queries, head_keys, head_values, head_grads, head_logsum, slope = items

        def per_block(carry, pair):
            key_total, value_total = carry
            block_queries, block_grads, block_logsum, start = pair
            scores = scores_of(block_queries, head_keys, slope, start)
            probs = jnp.exp(scores - block_logsum[:, None])
            d_probs = product_right(block_grads, head_values)
            row_total = jnp.sum(probs * d_probs, axis=-1, keepdims=True)
            d_scores = (probs * (d_probs - row_total) * 0.125).astype(jnp.bfloat16)
            d_block = product(d_scores, head_keys)
            key_total = key_total + product_left(d_scores, block_queries)
            value_total = value_total + product_left(probs.astype(jnp.bfloat16), block_grads)
            return ((key_total, value_total), d_block)

        empty = jnp.zeros(head_keys.shape, jnp.float32)
        (key_total, value_total), d_blocks = lax.scan(
            per_block, (empty, empty), (head_queries, head_grads, head_logsum, starts)
        )
        return (d_blocks.reshape(count, width), key_total, value_total)

    return lax.map(per_head, (query_blocks, keys, values, grad_blocks, logsum_blocks, slopes))


def body(
    tokens,
    w_query,
    w_key,
    w_value,
    w_out,
    gain_one,
    shift_one,
    w_gate,
    w_up,
    w_down,
    gain_two,
    shift_two,
    slopes,
    cotangent,
):
    shards = (
        w_query,
        w_key,
        w_value,
        w_out,
        gain_one,
        shift_one,
        w_gate,
        w_up,
        w_down,
        gain_two,
        shift_two,
    )
    full = (
        lax.all_gather(shards[0], "fsdp", axis=0, tiled=True),
        lax.all_gather(shards[1], "fsdp", axis=0, tiled=True),
        lax.all_gather(shards[2], "fsdp", axis=0, tiled=True),
        lax.all_gather(shards[3], "fsdp", axis=0, tiled=True),
        lax.all_gather(shards[4], "fsdp", axis=0, tiled=True),
        lax.all_gather(shards[5], "fsdp", axis=0, tiled=True),
        lax.all_gather(shards[6], "fsdp", axis=0, tiled=True),
        lax.all_gather(shards[7], "fsdp", axis=0, tiled=True),
        lax.all_gather(shards[8], "fsdp", axis=0, tiled=True),
        lax.all_gather(shards[9], "fsdp", axis=0, tiled=True),
        lax.all_gather(shards[10], "fsdp", axis=0, tiled=True),
    )
    (
        query_full,
        key_full,
        value_full,
        out_full,
        gain_a,
        shift_a,
        gate_full,
        up_full,
        down_full,
        gain_b,
        shift_b,
    ) = full
    groups = lax.axis_size("sp")
    source = tokens[0]
    count = source.shape[0]
    width = source.shape[1]
    local_heads = HEADS // groups
    head_width = local_heads * HEAD_DIM
    seq_rows = groups * count
    block = min(512, seq_rows)
    stacked = jnp.stack(
        (product(source, query_full), product(source, key_full), product(source, value_full))
    ).astype(jnp.bfloat16)
    stacked = stacked.reshape(3, count, groups, head_width)
    arrived = lax.all_to_all(stacked, "sp", split_axis=2, concat_axis=1, tiled=True).reshape(
        3, seq_rows, local_heads, HEAD_DIM
    )
    arrived = jnp.transpose(arrived, (0, 2, 1, 3))
    member = lax.axis_index("fsdp") % GROUP
    offset = (member * seq_rows).astype(jnp.float32)
    my_slopes = lax.dynamic_slice_in_dim(slopes, lax.axis_index("sp") * local_heads, local_heads)
    levels = GROUP.bit_length() - 1
    known = arrived[1:]
    for level in range(levels):
        other = from_partner(known, "fsdp", level)
        higher_half = member // 2**level % 2 == 1
        known = jnp.where(
            higher_half,
            jnp.concatenate((other, known), axis=2),
            jnp.concatenate((known, other), axis=2),
        )
    context, logsum = attend_forward(arrived[0], known[0], known[1], my_slopes, offset, block)
    sending = jnp.transpose(context.astype(jnp.bfloat16), (1, 0, 2)).reshape(
        groups, count, head_width
    )
    context_rows = lax.all_to_all(sending, "sp", split_axis=0, concat_axis=2, tiled=True).reshape(
        count, width
    )
    base = source.astype(jnp.float32)
    attended = product(context_rows, out_full)
    hidden, pull_one = jax.vjp(
        normalize, base + attended, gain_a.astype(jnp.float32), shift_a.astype(jnp.float32)
    )
    hidden_low = hidden.astype(jnp.bfloat16)
    gate = product(hidden_low, gate_full)
    upward = product(hidden_low, up_full)
    active_full, pull_act = jax.vjp(geglu, gate, upward)
    active = active_full.astype(jnp.bfloat16)
    branch = product(active, down_full)
    result, pull_two = jax.vjp(
        normalize, hidden + branch, gain_b.astype(jnp.float32), shift_b.astype(jnp.float32)
    )
    output = result.astype(jnp.bfloat16)[None]
    (
        query_back,
        key_back,
        value_back,
        out_back,
        unused_a,
        unused_b,
        gate_back,
        up_back,
        down_back,
        unused_c,
        unused_d,
    ) = full
    d_second, d_gain_b, d_shift_b = pull_two(cotangent[0].astype(jnp.float32))
    d_branch = d_second.astype(jnp.bfloat16)
    grad_down = product_left(active, d_branch)
    d_active = product_right(d_branch, down_back)
    d_gate, d_upward = pull_act(d_active)
    d_gate = d_gate.astype(jnp.bfloat16)
    d_upward = d_upward.astype(jnp.bfloat16)
    grad_gate = product_left(hidden_low, d_gate)
    grad_up = product_left(hidden_low, d_upward)
    d_hidden = d_second + product_right(d_gate, gate_back) + product_right(d_upward, up_back)
    d_first, d_gain_a, d_shift_a = pull_one(d_hidden)
    d_attended = d_first.astype(jnp.bfloat16)
    grad_out = product_left(context_rows, d_attended)
    d_context = product_right(d_attended, out_back).astype(jnp.bfloat16)
    d_heads = lax.all_to_all(
        d_context.reshape(count, groups, head_width), "sp", split_axis=1, concat_axis=0, tiled=True
    )
    d_heads = jnp.transpose(d_heads.reshape(seq_rows, local_heads, HEAD_DIM), (1, 0, 2))
    d_queries, d_keys, d_values = attend_backward(
        arrived[0], known[0], known[1], d_heads, logsum, my_slopes, offset, block
    )
    pending = jnp.stack((d_keys, d_values))
    for level in reversed(range(levels)):
        half = pending.shape[2] // 2
        lower = pending[:, :, :half]
        upper = pending[:, :, half:]
        higher_half = member // 2**level % 2 == 1
        staying = jnp.where(higher_half, upper, lower)
        leaving = jnp.where(higher_half, lower, upper)
        pending = staying + from_partner(leaving.astype(jnp.bfloat16), "fsdp", level).astype(
            leaving.dtype
        )
    d_all = jnp.concatenate((d_queries[None], pending), axis=0).astype(jnp.bfloat16)
    d_all = jnp.transpose(d_all, (0, 2, 1, 3)).reshape(3, groups, count, head_width)
    d_rows = lax.all_to_all(d_all, "sp", split_axis=1, concat_axis=3, tiled=True).reshape(
        3, count, width
    )
    grad_query = product_left(source, d_rows[0])
    grad_key = product_left(source, d_rows[1])
    grad_value = product_left(source, d_rows[2])
    d_tokens = (
        d_first
        + product_right(d_rows[0], query_back)
        + product_right(d_rows[1], key_back)
        + product_right(d_rows[2], value_back)
    )
    input_grad = d_tokens.astype(jnp.bfloat16)[None]
    norm_grads = jnp.stack((d_gain_a, d_shift_a, d_gain_b, d_shift_b), axis=1)
    owned = (
        lax.psum_scatter(grad_query, "fsdp", scatter_dimension=0, tiled=True),
        lax.psum_scatter(grad_key, "fsdp", scatter_dimension=0, tiled=True),
        lax.psum_scatter(grad_value, "fsdp", scatter_dimension=0, tiled=True),
        lax.psum_scatter(grad_out, "fsdp", scatter_dimension=0, tiled=True),
        lax.psum_scatter(grad_gate, "fsdp", scatter_dimension=0, tiled=True),
        lax.psum_scatter(grad_up, "fsdp", scatter_dimension=0, tiled=True),
        lax.psum_scatter(grad_down, "fsdp", scatter_dimension=0, tiled=True),
        lax.psum_scatter(norm_grads, "fsdp", scatter_dimension=0, tiled=True),
    )
    shares = (
        lax.psum(owned[0].astype(jnp.bfloat16), "sp").astype(jnp.float32),
        lax.psum(owned[1].astype(jnp.bfloat16), "sp").astype(jnp.float32),
        lax.psum(owned[2].astype(jnp.bfloat16), "sp").astype(jnp.float32),
        lax.psum(owned[3].astype(jnp.bfloat16), "sp").astype(jnp.float32),
        lax.psum(owned[4].astype(jnp.bfloat16), "sp").astype(jnp.float32),
        lax.psum(owned[5].astype(jnp.bfloat16), "sp").astype(jnp.float32),
        lax.psum(owned[6].astype(jnp.bfloat16), "sp").astype(jnp.float32),
        lax.psum(owned[7].astype(jnp.bfloat16), "sp").astype(jnp.float32),
    )
    norm_share = shares[7]
    return (
        output,
        input_grad,
        shares[0],
        shares[1],
        shares[2],
        shares[3],
        norm_share[:, 0],
        norm_share[:, 1],
        shares[4],
        shares[5],
        shares[6],
        norm_share[:, 2],
        norm_share[:, 3],
    )


def solution(mesh):
    placed = (
        P("fsdp", "sp", None),
        P("fsdp", None),
        P("fsdp", None),
        P("fsdp", None),
        P("fsdp", None),
        P("fsdp"),
        P("fsdp"),
        P("fsdp", None),
        P("fsdp", None),
        P("fsdp", None),
        P("fsdp"),
        P("fsdp"),
        P(),
        P("fsdp", "sp", None),
    )
    return jax.shard_map(
        body,
        mesh=mesh,
        in_specs=placed,
        out_specs=(
            P("fsdp", "sp", None),
            P("fsdp", "sp", None),
            P("fsdp", None),
            P("fsdp", None),
            P("fsdp", None),
            P("fsdp", None),
            P("fsdp"),
            P("fsdp"),
            P("fsdp", None),
            P("fsdp", None),
            P("fsdp", None),
            P("fsdp"),
            P("fsdp"),
        ),
        check_vma=False,
    )
```

profile of v0, /device:TPU:0, one launch (start us, length us, event | category | flops | bytes accessed | tf_op | source)
XLA Modules:
  0.0 1951.3 jit_solution(3255887086396379797)
XLA Ops:
  11.2 42.8 %all-gather.8.cloned.1.call-done = bf16[768,768]{1,0:T(8,128)(2,1)} async-done(((bf16[96,768]{1,0:T(8,128)(2,1)}), bf16[768,768]{1,0:T(8,128)(2,1)}) %all-gather.8.cloned.1.call-update) | async-done | bytes 1179664 | tf_op jit(solution)/shard_map/all_gather | solution.py:140
  55.6 40.5 %all-gather.10.cloned.1.call-done = bf16[768,768]{1,0:T(8,128)(2,1)} async-done(((bf16[96,768]{1,0:T(8,128)(2,1)}), bf16[768,768]{1,0:T(8,128)(2,1)}) %all-gather.10.cloned.1.call-update) | async-done | bytes 1179664 | tf_op jit(solution)/shard_map/all_gather | solution.py:141
  97.7 40.4 %all-gather.12.cloned.1.call-done = bf16[768,768]{1,0:T(8,128)(2,1)} async-done(((bf16[96,768]{1,0:T(8,128)(2,1)}), bf16[768,768]{1,0:T(8,128)(2,1)}) %all-gather.12.cloned.1.call-update) | async-done | bytes 1179664 | tf_op jit(solution)/shard_map/all_gather | solution.py:142
  143.3 24.9 %all_to_all.60 = bf16[3,384,4,192]{1,3,0,2:T(8,128)(2,1)S(1)} all-to-all(bf16[3,384,4,192]{1,3,0,2:T(8,128)(2,1)S(1)} %copy.82), channel_id=1, replica_groups=mesh['sp'=4,'fsdp'=8] {'sp'}, dimensions={2} | all-to-all | bytes 3538944 | tf_op jit(solution)/shard_map/all_to_all | solution.py:177
  171.5 33.3 %collective-permute-done = bf16[2,3,1536,64]{2,3,1,0:T(8,128)(2,1)} collective-permute-done((bf16[2,3,1536,64]{2,3,1,0:T(8,128)(2,1)S(1)}, bf16[2,3,1536,64]{2,3,1,0:T(8,128)(2,1)}, u32[]{:S(2)}, u32[]{:S(2)}) %collective-permute-start) | collective-permute-done | bytes 1179680 | tf_op jit(solution)/shard_map/ppermute | solution.py:15
  210.7 92.7 %collective-permute-done.1 = bf16[2,3,3072,64]{2,3,1,0:T(8,128)(2,1)} collective-permute-done((bf16[2,3,3072,64]{2,3,1,0:T(8,128)(2,1)S(1)}, bf16[2,3,3072,64]{2,3,1,0:T(8,128)(2,1)}, u32[]{:S(2)}, u32[]{:S(2)}) %collective-permute-start.1) | collective-permute-done | bytes 2359328 | tf_op jit(solution)/shard_map/ppermute | solution.py:15
  318.6 187.3 %while.58 = (s32[]{:T(128)}, bf16[3,3,512,64]{2,3,1,0:T(8,128)(2,1)}, f32[3,3,512]{2,1,0:T(4,128)}, bf16[3,3,512,64]{3,2,1,0:T(8,128)(2,1)}, bf16[3,6144,64]{2,1...) while((s32[]{:T(128)}, ...), condition=%wide.region_5.6_spmd.clone, body=%wide.region_0.5_spmd.clone.sunk | while | flops 839909376 | bytes 94676872 | solution.py:73
  322.8 55.2 %while.61 = (s32[]{:T(128)}, bf16[3,512,64]{1,2,0:T(8,128)(2,1)}, f32[3,512]{1,0:T(4,128)}, bf16[3,512,64]{2,1,0:T(8,128)(2,1)S(1)}, bf16[6144,64]{1,0:T(8,128)(...) while((s32[]{:T(128)}, bf16[3,512,64]{1,2,0:T(8,128)(2,1)}, ...), condition=%wide.region_4.4_spmd, body=%wide.region_1.3_spmd.sunk | while | flops 839909376 | bytes 90727064 | solution.py:71
  385.1 55.5 %while.61 = (s32[]{:T(128)}, bf16[3,512,64]{1,2,0:T(8,128)(2,1)}, f32[3,512]{1,0:T(4,128)}, bf16[3,512,64]{2,1,0:T(8,128)(2,1)S(1)}, bf16[6144,64]{1,0:T(8,128)(...) while((s32[]{:T(128)}, bf16[3,512,64]{1,2,0:T(8,128)(2,1)}, ...), condition=%wide.region_4.4_spmd, body=%wide.region_1.3_spmd.sunk | while | flops 839909376 | bytes 90727064 | solution.py:71
  447.7 55.2 %while.61 = (s32[]{:T(128)}, bf16[3,512,64]{1,2,0:T(8,128)(2,1)}, f32[3,512]{1,0:T(4,128)}, bf16[3,512,64]{2,1,0:T(8,128)(2,1)S(1)}, bf16[6144,64]{1,0:T(8,128)(...) while((s32[]{:T(128)}, bf16[3,512,64]{1,2,0:T(8,128)(2,1)}, ...), condition=%wide.region_4.4_spmd, body=%wide.region_1.3_spmd.sunk | while | flops 839909376 | bytes 90727064 | solution.py:71
  513.8 19.8 %all-reduce.4 = (bf16[768]{0:T(1024)(128)(2,1)S(1)}, bf16[768]{0:T(1024)(128)(2,1)S(1)}, bf16[768]{0:T(1024)(128)(2,1)S(1)}, bf16[768]{0:T(1024)(128)(2,1)S(1)}) all-reduce(bf16[768]{0:T(1024)(128)(2,1)S(1)} %dynamic-update-slice.1, bf16[768]{0:T(1024)(128)(2,1)S(1)} %dynamic-update-slice, ...), channel_id=1, replica_groups=mesh['sp'=4,'fsdp'=8] {'fsdp'}, use_global_device_ids=true, to_apply=%add.1 | all-reduce | flops 3072 | bytes 12288
  543.2 15.1 multiply_convert_fusion.2
  566.3 10.0 multiply_convert_fusion.1
  590.6 9.4 all-to-all-done.2
  602.3 355.6 %while.60 = (s32[]{:T(128)}, bf16[3,1536,64]{1,2,0:T(8,128)(2,1)}, f32[3,6144,64]{1,2,0:T(8,128)}, f32[3,6144,64]{1,2,0:T(8,128)}, bf16[3,3,512,64]{3,2,1,0:T(8,...) while((s32[]{:T(128)}, bf16[3,1536,64]{1,2,0:T(8,128)(2,1)}, ...), condition=%wide.region_18.19_spmd.clone, body=%wide.region_14.18_spmd.clone.sunk | while | flops 2055733248 | bytes 229143760 | solution.py:107
  612.3 103.5 %while.62 = (s32[]{:T(128)}, f32[6144,64]{0,1:T(8,128)}, f32[6144,64]{0,1:T(8,128)}, bf16[3,512,64]{1,2,0:T(8,128)(2,1)S(1)}, bf16[3,512,64]{2,1,0:T(8,128)(2,1)...) while((s32[]{:T(128)}, f32[6144,64]{0,1:T(8,128)}, ...), condition=%wide.region_17.17_spmd.clone, body=%wide.region_15.16_spmd.clone.sunk | while | flops 2055733248 | bytes 217726736 | solution.py:102
  730.9 103.5 %while.62 = (s32[]{:T(128)}, f32[6144,64]{0,1:T(8,128)}, f32[6144,64]{0,1:T(8,128)}, bf16[3,512,64]{1,2,0:T(8,128)(2,1)S(1)}, bf16[3,512,64]{2,1,0:T(8,128)(2,1)...) while((s32[]{:T(128)}, f32[6144,64]{0,1:T(8,128)}, ...), condition=%wide.region_17.17_spmd.clone, body=%wide.region_15.16_spmd.clone.sunk | while | flops 2055733248 | bytes 217726736 | solution.py:102
  736.1 6.8 multiply_reduce_fusion.6
  849.3 103.5 %while.62 = (s32[]{:T(128)}, f32[6144,64]{0,1:T(8,128)}, f32[6144,64]{0,1:T(8,128)}, bf16[3,512,64]{1,2,0:T(8,128)(2,1)S(1)}, bf16[3,512,64]{2,1,0:T(8,128)(2,1)...) while((s32[]{:T(128)}, f32[6144,64]{0,1:T(8,128)}, ...), condition=%wide.region_17.17_spmd.clone, body=%wide.region_15.16_spmd.clone.sunk | while | flops 2055733248 | bytes 217726736 | solution.py:102
  966.1 70.1 %collective-permute-done.2 = bf16[2,3,3072,64]{2,3,1,0:T(8,128)(2,1)S(1)} collective-permute-done((bf16[2,3,3072,64]{2,3,1,0:T(8,128)(2,1)}, bf16[2,3,3072,64]{2,3,1,0:T(8,128)(2,1)S(1)}, u32[]{:S(2)}, u32[]{:S(2)}) %collective-permute-start.2) | collective-permute-done | bytes 2359328 | tf_op jit(solution)/shard_map/ppermute | solution.py:15
  1040.8 26.0 %collective-permute-done.3 = bf16[2,3,1536,64]{2,3,1,0:T(8,128)(2,1)S(1)} collective-permute-done((bf16[2,3,1536,64]{2,3,1,0:T(8,128)(2,1)S(1)}, bf16[2,3,1536,64]{2,3,1,0:T(8,128)(2,1)S(1)}, u32[]{:S(2)}, u32[]{:S(2)}) %collective-permute-start.3) | collective-permute-done | bytes 1179680 | tf_op jit(solution)/shard_map/ppermute | solution.py:15
  1071.2 24.6 %all_to_all.61 = bf16[3,4,384,192]{2,3,0,1:T(8,128)(2,1)S(1)} all-to-all(bf16[3,4,384,192]{2,3,0,1:T(8,128)(2,1)S(1)} %copy.96), channel_id=1, replica_groups=mesh['sp'=4,'fsdp'=8] {'sp'}, dimensions={1} | all-to-all | bytes 3538944 | tf_op jit(solution)/shard_map/all_to_all | solution.py:263
  1113.6 8.4 fusion.54
  1123.1 6.8 fusion.65
  1140.9 26.9 %reduce-scatter.25.cloned.1.call-done = f32[96,768]{1,0:T(8,128)} async-done(((f32[768,768]{1,0:T(8,128)}), f32[96,768]{1,0:T(8,128)}) %reduce-scatter.25.cloned.1.call-update) | async-done | bytes 294928
  1169.6 69.6 %reduce-scatter.27.cloned.1.call-done = f32[96,768]{1,0:T(8,128)} async-done(((f32[768,768]{1,0:T(8,128)}), f32[96,768]{1,0:T(8,128)}) %reduce-scatter.27.cloned.1.call-update) | async-done | bytes 294928
  1241.0 70.0 %reduce-scatter.29.cloned.1.call-done = f32[96,768]{1,0:T(8,128)} async-done(((f32[768,768]{1,0:T(8,128)}), f32[96,768]{1,0:T(8,128)}) %reduce-scatter.29.cloned.1.call-update) | async-done | bytes 294928
  1312.7 164.2 %reduce-scatter.23.cloned.1.call-done = f32[384,768]{1,0:T(8,128)} async-done(((f32[3072,768]{1,0:T(8,128)}), f32[384,768]{1,0:T(8,128)}) %reduce-scatter.23.cloned.1.call-update) | async-done | bytes 1179664 | tf_op jit(solution)/shard_map/reduce_scatter | solution.py:284
  1479.0 164.1 %reduce-scatter.19.cloned.1.call-done = f32[96,3072]{1,0:T(8,128)} async-done(((f32[768,3072]{1,0:T(8,128)}), f32[96,3072]{1,0:T(8,128)}) %reduce-scatter.19.cloned.1.call-update) | async-done | bytes 1179664 | tf_op jit(solution)/shard_map/reduce_scatter | solution.py:282
  1645.3 163.9 %reduce-scatter.21.cloned.1.call-done = f32[96,3072]{1,0:T(8,128)} async-done(((f32[768,3072]{1,0:T(8,128)}), f32[96,3072]{1,0:T(8,128)}) %reduce-scatter.21.cloned.1.call-update) | async-done | bytes 1179664 | tf_op jit(solution)/shard_map/reduce_scatter | solution.py:283
  1811.4 62.0 %reduce-scatter.31.cloned.1.call-done = f32[96,4]{1,0:T(8,128)} async-done(((f32[768,4]{1,0:T(8,128)}), f32[96,4]{1,0:T(8,128)}) %reduce-scatter.31.cloned.1.call-update) | async-done | bytes 1552
  1885.2 50.4 %all-reduce.8.cloned.1.call-done = (bf16[96,768]{0,1:T(8,128)(2,1)}, bf16[96,768]{0,1:T(8,128)(2,1)}, bf16[96,768]{0,1:T(8,128)(2,1)}, bf16[96,768]{1,0:T(8,128)...) async-done(((bf16[96,768]{0,1:T(8,128)(2,1)}, bf16[96,768]{0,1:T(8,128)(2,1)}, bf16[96,768]{0,1:T(8,128)(2,1)}, ...) | async-done | bytes 2359312 | tf_op jit(solution)/shard_map/psum | solution.py:288
  (545 shorter events, 692.1 us)
Async XLA Ops:
  7.2 46.8 %all-gather.8.cloned.1.call-start = ((), (), s32[]{:S(2)}) async-start(), calls=%async_computation.12 | async-start | bytes 1327104 | tf_op jit(solution)/shard_map/all_gather | solution.py:140
  7.9 88.1 %all-gather.10.cloned.1.call-start = ((), (), s32[]{:S(2)}) async-start(), calls=%async_computation.13 | async-start | bytes 1327104 | tf_op jit(solution)/shard_map/all_gather | solution.py:141
  8.7 129.4 %all-gather.12.cloned.1.call-start = ((), (), s32[]{:S(2)}) async-start(), calls=%async_computation.14 | async-start | bytes 1327104 | tf_op jit(solution)/shard_map/all_gather | solution.py:142
  9.4 524.3 %all-gather.14.cloned.1.call-start = ((), (), s32[]{:S(2)}) async-start(), calls=%async_computation.15 | async-start | bytes 1327104 | tf_op jit(solution)/shard_map/all_gather | solution.py:143
  10.0 526.5 %all-gather.16.cloned.1.call-start = ((), (), s32[]{:S(2)}) async-start(), calls=%async_computation.16 | async-start | bytes 5308416 | tf_op jit(solution)/shard_map/all_gather | solution.py:146
  10.6 532.6 %all-gather.18.cloned.1.call-start = ((), (), s32[]{:S(2)}) async-start(), calls=%async_computation.17 | async-start | bytes 5308416 | tf_op jit(solution)/shard_map/all_gather | solution.py:147
  11.1 547.2 %all-gather.20.cloned.1.call-start = ((), (), s32[]{:S(2)}) async-start(), calls=%async_computation.18 | async-start | bytes 5308416 | tf_op jit(solution)/shard_map/all_gather | solution.py:148
  96.0 44.4 %copy-start.7 = (bf16[1,384,768]{2,1,0:T(8,128)(2,1)S(1)}, bf16[1,384,768]{2,1,0:T(8,128)(2,1)}, u32[]{:S(2)}) copy-start(bf16[1,384,768]{2,1,0:T(8,128)(2,1)} %param.22) | copy-start | bytes 1769476
  170.4 34.4 %collective-permute-start = (bf16[2,3,1536,64]{2,3,1,0:T(8,128)(2,1)S(1)}, bf16[2,3,1536,64]{2,3,1,0:T(8,128)(2,1)}, u32[]{:S(2)}, u32[]{:S(2)}) collective-permute-start(bf16[2,3,1536,64]{2,3,1,0:T(8,128)(2,1)S(1)} %slice.70), channel_id=1, source_target_pairs={{0,1},{1,0},{2,3},{3,2},{4,5},{5,4},{6,7},{7,6},{8,9},{9,8},{10,11... | collective-permute-start | bytes 3538952 | tf_op jit(solution)/shard_map/ppermute | solution.py:15
  171.5 36.7 %copy-start.37 = (f32[12]{0:T(128)S(1)}, f32[12]{0:T(128)}, u32[]{:S(2)}) copy-start(f32[12]{0:T(128)} %param.34) | copy-start | bytes 148
  207.1 96.3 %collective-permute-start.1 = (bf16[2,3,3072,64]{2,3,1,0:T(8,128)(2,1)S(1)}, bf16[2,3,3072,64]{2,3,1,0:T(8,128)(2,1)}, u32[]{:S(2)}, u32[]{:S(2)}) collective-permute-start(bf16[2,3,3072,64]{2,3,1,0:T(8,128)(2,1)S(1)} %maximum_select_fusion.1), channel_id=1, source_target_pairs={{0,2},{1,3},{2,0},{3,1},{4,6},{5,7},{6,4},{7,5},{8,10},{9,11},{10,... | collective-permute-start | bytes 7077896 | tf_op jit(solution)/shard_map/ppermute | solution.py:15
  505.9 27.8 %copy-start.8 = (bf16[1,384,768]{2,1,0:T(8,128)(2,1)S(1)}, bf16[1,384,768]{2,1,0:T(8,128)(2,1)}, u32[]{:S(2)}) copy-start(bf16[1,384,768]{2,1,0:T(8,128)(2,1)} %param.22) | copy-start | bytes 1769476
  508.1 25.6 %all-to-all-start.1 = ((bf16[4,384,192]{1,2,0:T(8,128)(2,1)}), bf16[4,384,192]{1,2,0:T(8,128)(2,1)S(1)}, u32[]{:S(2)}, u32[]{:S(2)}) async-start(bf16[4,384,192]{1,2,0:T(8,128)(2,1)} %copy.88), calls=%async_computation.1 | async-start | bytes 1179648 | tf_op jit(solution)/shard_map/all_to_all | solution.py:198
  587.1 13.0 all-to-all-start.2
  590.6 548.7 %reduce-scatter.17.cloned.1.call-start = ((), (), s32[]{:S(2)}) async-start(), calls=%async_computation.19 | async-start | bytes 2654208 | tf_op jit(solution)/shard_map/reduce_scatter | solution.py:281
  666.8 11.7 copy-start.1
  701.4 11.7 copy-start.1
  785.3 11.7 copy-start.1
  820.0 11.7 copy-start.1
  903.8 11.7 copy-start.1
  938.4 11.7 copy-start.1
  963.6 72.7 %collective-permute-start.2 = (bf16[2,3,3072,64]{2,3,1,0:T(8,128)(2,1)}, bf16[2,3,3072,64]{2,3,1,0:T(8,128)(2,1)S(1)}, u32[]{:S(2)}, u32[]{:S(2)}) collective-permute-start(bf16[2,3,3072,64]{2,3,1,0:T(8,128)(2,1)} %select_convert_fusion), channel_id=1, source_target_pairs={{0,2},{1,3},{2,0},{3,1},{4,6},{5,7},{6,4},{7,5},{8,10},{9,11},{10,... | collective-permute-start | bytes 7077896 | tf_op jit(solution)/shard_map/ppermute | solution.py:15
  966.1 201.7 %reduce-scatter.25.cloned.1.call-start = ((), (), s32[]{:S(2)}) async-start(), calls=%async_computation.23 | async-start | bytes 2654208
  1040.7 26.7 %copy-start.25 = (bf16[3,1536,64]{1,2,0:T(8,128)(2,1)S(1)}, bf16[3,1536,64]{1,2,0:T(8,128)(2,1)}, u32[]{:S(2)}) copy-start(bf16[3,1536,64]{1,2,0:T(8,128)(2,1)} %get-tuple-element.219) | copy-start | bytes 1769476
  1040.7 26.0 %collective-permute-start.3 = (bf16[2,3,1536,64]{2,3,1,0:T(8,128)(2,1)S(1)}, bf16[2,3,1536,64]{2,3,1,0:T(8,128)(2,1)S(1)}, u32[]{:S(2)}, u32[]{:S(2)}) collective-permute-start(bf16[2,3,1536,64]{2,3,1,0:T(8,128)(2,1)S(1)} %select_convert_fusion.1), channel_id=1, source_target_pairs={{0,1},{1,0},{2,3},{3,2},{4,5},{5,4},{6,7},{7,6},{8,9},{9,8},{10,11... | collective-permute-start | bytes 3538952 | tf_op jit(solution)/shard_map/ppermute | solution.py:15
  1102.3 136.8 %reduce-scatter.27.cloned.1.call-start = ((), (), s32[]{:S(2)}) async-start(), calls=%async_computation.24 | async-start | bytes 2654208
  1107.7 203.2 %reduce-scatter.29.cloned.1.call-start = ((), (), s32[]{:S(2)}) async-start(), calls=%async_computation.25 | async-start | bytes 2654208
  1113.0 363.9 %reduce-scatter.23.cloned.1.call-start = ((), (), s32[]{:S(2)}) async-start(), calls=%async_computation.22 | async-start | bytes 10616832 | tf_op jit(solution)/shard_map/reduce_scatter | solution.py:284
  1122.1 521.1 %reduce-scatter.19.cloned.1.call-start = ((), (), s32[]{:S(2)}) async-start(), calls=%async_computation.20 | async-start | bytes 10616832 | tf_op jit(solution)/shard_map/reduce_scatter | solution.py:282
  1129.9 679.3 %reduce-scatter.21.cloned.1.call-start = ((), (), s32[]{:S(2)}) async-start(), calls=%async_computation.21 | async-start | bytes 10616832 | tf_op jit(solution)/shard_map/reduce_scatter | solution.py:283
  1136.7 736.6 %reduce-scatter.31.cloned.1.call-start = ((), (), s32[]{:S(2)}) async-start(), calls=%async_computation.26 | async-start | bytes 442368
  1139.0 796.7 %all-reduce.8.cloned.1.call-start = ((), (), s32[]{:S(2)}) async-start(), calls=%async_computation.27 | async-start | bytes 5013504 | tf_op jit(solution)/shard_map/psum | solution.py:288
  (81 other events, 378.1 us)
Sparse Core Ops, SparseCore 0:
  10.2 43.7 all-gather.7
  56.2 39.8 all-gather.9
  98.2 39.8 all-gather.11
  140.1 39.8 all-gather.13
  182.0 119.6 all-gather.15
  303.7 81.0 all-gather.17
  387.0 77.9 all-gather.19
  966.2 82.8 reduce-scatter.16
  1102.5 65.3 reduce-scatter.24
  1171.2 67.9 reduce-scatter.26
  1242.7 68.1 reduce-scatter.28
  1314.4 162.4 reduce-scatter.22
  1480.5 162.5 reduce-scatter.18
  1646.6 162.5 reduce-scatter.20
  1812.9 60.4 reduce-scatter.30
  1877.3 58.3 all-reduce.7
where the time goes:
time: 1960 us; the launch traced here: 1950 us
  waiting for transfers between devices  1130 us (58%)
  matrix products  388 us (20%)
  local copies, waits for them, and re-layouts  233 us (12%)
  other arithmetic  99 us (5%)
  blocking collectives  75 us (4%)
    unnamed x20, waiting for transfers between devices  232 us
    ppermute x4, waiting for transfers between devices, from_partner(): lax.ppermute(array, axis, [(i, i ^ 1 << distance) for i in range(lax.axis...  222 us
    reduce_scatter x1, waiting for transfers between devices, body(): lax.psum_scatter(grad_down, 'fsdp', scatter_dimension=0, tiled=True)  164 us
    reduce_scatter x1, waiting for transfers between devices, body(): lax.psum_scatter(grad_gate, 'fsdp', scatter_dimension=0, tiled=True)  164 us
    reduce_scatter x1, waiting for transfers between devices, body(): lax.psum_scatter(grad_up, 'fsdp', scatter_dimension=0, tiled=True)  164 us
    dot_general x34, matrix products, product_right(): lax.dot_general(left, right, (((1,), (1,)), ((), ())), preferred_element_...  148 us
    dot_general x25, matrix products, product(): return jnp.dot(left, right, preferred_element_type=jnp.float32)  144 us
    dot_general x25, matrix products, product_left(): lax.dot_general(left, right, (((0,), (0,)), ((), ())), preferred_element_...  95.9 us
  transfers between devices with their start and end apart: 22, of which 16 were waited for; matrix products, arithmetic and copies ran while one was open for 15% of the time, Pallas kernels for 0%

commit v1 on v0

v1 whole, which is shorter than its diff:
```python
import functools

import jax
import jax.numpy as jnp
from jax import lax
from jax.experimental import pallas as pl
from jax.experimental.pallas import tpu as pltpu
from jax.sharding import PartitionSpec as P

HEADS = 12
HEAD_DIM = 64
GROUP = 4
VALUE_ROWS = 80
VMEM_BYTES = 50 * 1024 * 1024


EPS = 1e-12


def from_partner(array, axis, distance):
    return lax.ppermute(array, axis, [(i, i ^ distance) for i in range(lax.axis_size(axis))])


def from_sp(array, distance):
    return from_partner(array, "sp", distance)


def normalize(residual_sum, gain, shift):
    average = jnp.mean(residual_sum, axis=-1, keepdims=True)
    centred = residual_sum - average
    spread = jnp.mean(centred * centred, axis=-1, keepdims=True)
    return centred * lax.rsqrt(spread + EPS) * gain + shift


def geglu(gate, upward):
    return jax.nn.gelu(gate, approximate=False) * upward


def product(left, right):
    return jnp.dot(left, right, preferred_element_type=jnp.float32)


def product_left(left, right):
    return lax.dot_general(
        left, right, (((0,), (0,)), ((), ())), preferred_element_type=jnp.float32
    )


def product_right(left, right):
    return lax.dot_general(
        left, right, (((1,), (1,)), ((), ())), preferred_element_type=jnp.float32
    )


def ramp(block):
    shape = (block, block)
    down = lax.broadcasted_iota(jnp.int32, shape, 0)
    across = lax.broadcasted_iota(jnp.int32, shape, 1)
    return (down - across).astype(jnp.float32)


def forward_kernel(block, slopes_ref, bases_ref, q_ref, k_ref, v_ref, o_ref, lse_ref, tile_ref):
    head = pl.program_id(0)
    place = pl.program_id(1)
    slope = slopes_ref[head]

    @pl.when(place == 0)
    def _():
        tile_ref[...] = ramp(block) * slope

    queries = q_ref[0]
    start = bases_ref[place]

    def step(chunk, carry):
        highest, total = carry
        rows = pl.ds(pl.multiple_of(chunk * block, block), block)
        raw = jnp.dot(k_ref[0, rows, :], queries, preferred_element_type=jnp.float32)
        shift = slope * (bases_ref[chunk] - start)
        scores = raw - jnp.abs(tile_ref[...] + shift)
        newest = jnp.maximum(highest, jnp.max(scores, axis=0, keepdims=True))
        raised = jnp.exp(scores - newest).astype(jnp.bfloat16)
        part = jnp.dot(v_ref[0, :, rows], raised, preferred_element_type=jnp.float32)
        return newest, total * jnp.exp(highest - newest) + part

    chunks = k_ref.shape[1] // block
    highest = jnp.full((1, block), -jnp.inf, jnp.float32)
    total = jnp.zeros((VALUE_ROWS, block), jnp.float32)
    highest, total = lax.fori_loop(0, chunks, step, (highest, total), unroll=4)
    sums = total[HEAD_DIM : HEAD_DIM + 1]
    o_ref[0] = total[:HEAD_DIM] / sums
    lse_ref[0] = highest + jnp.log(sums)


def backward_kernel(
    block,
    slopes_ref,
    bases_ref,
    qt_ref,
    q_ref,
    gt_ref,
    g_ref,
    o_ref,
    lse_ref,
    k_ref,
    kt_ref,
    v_ref,
    dq_ref,
    dk_ref,
    dv_ref,
    tile_ref,
):
    head = pl.program_id(0)
    place = pl.program_id(1)
    slope = slopes_ref[head]

    @pl.when(place == 0)
    def _():
        tile_ref[...] = ramp(block) * slope
        dk_ref[...] = jnp.zeros_like(dk_ref)
        dv_ref[...] = jnp.zeros_like(dv_ref)

    start = bases_ref[place]
    queries_t = qt_ref[0]
    grads_t = gt_ref[0]
    logsum = lse_ref[0]
    means = jnp.sum(grads_t.astype(jnp.float32) * o_ref[0], axis=0, keepdims=True)

    def step(chunk, total):
        rows = pl.ds(pl.multiple_of(chunk * block, block), block)
        raw = jnp.dot(k_ref[0, rows, :], queries_t, preferred_element_type=jnp.float32)
        shift = slope * (bases_ref[chunk] - start)
        probs = jnp.exp(raw - jnp.abs(tile_ref[...] + shift) - logsum)
        d_probs = jnp.dot(v_ref[0, rows, :], grads_t, preferred_element_type=jnp.float32)
        d_scores = (probs * (d_probs - means)).astype(jnp.bfloat16)
        dv_ref[0, rows, :] += jnp.dot(
            probs.astype(jnp.bfloat16), g_ref[0], preferred_element_type=jnp.float32
        )
        dk_ref[0, rows, :] += jnp.dot(d_scores, q_ref[0], preferred_element_type=jnp.float32)
        return total + jnp.dot(kt_ref[0, :, rows], d_scores, preferred_element_type=jnp.float32)

    chunks = k_ref.shape[1] // block
    total = jnp.zeros((HEAD_DIM, block), jnp.float32)
    total = lax.fori_loop(0, chunks, step, total, unroll=2)
    dq_ref[0] = total * 0.125


def scalars():
    return pl.BlockSpec(memory_space=pltpu.SMEM)


def across(rows, block):
    return pl.BlockSpec((1, rows, block), lambda h, i: (h, 0, i))


def down(block):
    return pl.BlockSpec((1, block, HEAD_DIM), lambda h, i: (h, i, 0))


def whole(rows, columns):
    return pl.BlockSpec((1, rows, columns), lambda h, i: (h, 0, 0))


def attend_forward(slopes, bases, queries_t, keys, values_t, block):
    heads, width, count = queries_t.shape
    length = keys.shape[1]
    work = heads * count * length
    return pl.pallas_call(
        functools.partial(forward_kernel, block),
        grid=(heads, count // block),
        in_specs=[
            scalars(),
            scalars(),
            across(width, block),
            whole(length, width),
            whole(VALUE_ROWS, length),
        ],
        out_specs=[across(width, block), across(1, block)],
        out_shape=[
            jax.ShapeDtypeStruct((heads, width, count), jnp.float32),
            jax.ShapeDtypeStruct((heads, 1, count), jnp.float32),
        ],
        scratch_shapes=[pltpu.VMEM((block, block), jnp.float32)],
        compiler_params=pltpu.CompilerParams(vmem_limit_bytes=VMEM_BYTES),
        cost_estimate=pl.CostEstimate(
            flops=16 * work * width, bytes_accessed=16 * heads * length * width, transcendentals=work
        ),
    )(slopes, bases, queries_t, keys, values_t)


def attend_backward(
    slopes, bases, queries_t, queries, grads_t, grads, context_t, logsum, keys, keys_t, values, block
):
    heads, width, count = queries_t.shape
    length = keys.shape[1]
    work = heads * count * length
    return pl.pallas_call(
        functools.partial(backward_kernel, block),
        grid=(heads, count // block),
        in_specs=[
            scalars(),
            scalars(),
            across(width, block),
            down(block),
            across(width, block),
            down(block),
            across(width, block),
            across(1, block),
            whole(length, width),
            whole(width, length),
            whole(length, width),
        ],
        out_specs=[across(width, block), whole(length, width), whole(length, width)],
        out_shape=[
            jax.ShapeDtypeStruct((heads, width, count), jnp.float32),
            jax.ShapeDtypeStruct((heads, length, width), jnp.float32),
            jax.ShapeDtypeStruct((heads, length, width), jnp.float32),
        ],
        scratch_shapes=[pltpu.VMEM((block, block), jnp.float32)],
        compiler_params=pltpu.CompilerParams(vmem_limit_bytes=VMEM_BYTES),
        cost_estimate=pl.CostEstimate(
            flops=40 * work * width, bytes_accessed=32 * heads * length * width, transcendentals=work
        ),
    )(slopes, bases, queries_t, queries, grads_t, grads, context_t, logsum, keys, keys_t, values)


def gather_rows(shard):
    return lax.all_gather(shard, "fsdp", axis=0, tiled=True)


def four_from_sp(mine):
    opposite = from_sp(mine, 2)
    return (mine, from_sp(mine, 1), opposite, from_sp(opposite, 1))


def sum_to_quarter(parts):
    low = [part.astype(jnp.bfloat16) for part in parts]
    near = parts[0] + from_sp(low[1], 1).astype(jnp.float32)
    far = parts[2] + from_sp(low[3], 1).astype(jnp.float32)
    return near + from_sp(far.astype(jnp.bfloat16), 2).astype(jnp.float32)


def scatter_rows(quarter):
    low = lax.psum_scatter(
        quarter.astype(jnp.bfloat16), "fsdp", scatter_dimension=0, tiled=True
    )
    return lax.all_gather(low, "sp", axis=0, tiled=False).astype(jnp.float32)


def body(
    tokens,
    w_query,
    w_key,
    w_value,
    w_out,
    gain_one,
    shift_one,
    w_gate,
    w_up,
    w_down,
    gain_two,
    shift_two,
    slopes,
    cotangent,
):
    groups = lax.axis_size("sp")
    owners = lax.axis_size("fsdp")
    me = lax.axis_index("sp")
    source = tokens[0]
    count, width = source.shape
    head_width = HEADS // groups * HEAD_DIM
    local_heads = HEADS // groups
    seq_rows = groups * count
    hidden_units = w_gate.shape[1]
    hidden_part = hidden_units // groups
    piece_part = hidden_part // owners
    bf16 = jnp.bfloat16
    f32 = jnp.float32

    def my_columns(weight):
        return lax.dynamic_slice_in_dim(weight, me * head_width, head_width, axis=1)

    def my_units(weight):
        split = weight.reshape(weight.shape[0], owners, groups, piece_part)
        return lax.dynamic_index_in_dim(split, me, 2, keepdims=False).reshape(-1, hidden_part)

    w_three = gather_rows(
        jnp.concatenate((my_columns(w_query), my_columns(w_key), my_columns(w_value)), axis=1)
    )
    threes = four_from_sp(w_three)
    vectors = jnp.stack((gain_one, shift_one, gain_two, shift_two), axis=1)
    my_down = lax.dynamic_slice_in_dim(w_down, me * piece_part, piece_part, axis=0)
    w_pairs = gather_rows(jnp.concatenate((my_units(w_gate), my_units(w_up)), axis=1))
    w_rest = gather_rows(my_down)
    out_full = gather_rows(w_out)
    vectors_full = gather_rows(vectors).astype(f32)
    gain_a, shift_a, gain_b, shift_b = [vectors_full[:, i] for i in range(4)]
    pair_parts = four_from_sp(w_pairs)
    gate_full = jnp.concatenate([part[:, :hidden_part] for part in pair_parts], axis=1)
    up_full = jnp.concatenate([part[:, hidden_part:] for part in pair_parts], axis=1)
    down_full = jnp.concatenate(four_from_sp(w_rest), axis=0)

    projected = [product(source, weight).astype(bf16) for weight in threes]
    arrived = [projected[0]] + [from_sp(projected[p], p) for p in range(1, groups)]
    arrived = jnp.concatenate(arrived, axis=0)
    member = lax.axis_index("fsdp") % GROUP
    my_slopes = lax.dynamic_slice_in_dim(slopes, me * local_heads, local_heads)
    chunk = jnp.arange(groups, dtype=jnp.int32) ^ me
    piece = jnp.arange(GROUP, dtype=jnp.int32) ^ member
    bases = (piece[:, None] * seq_rows + chunk[None, :] * count).reshape(-1).astype(f32)

    pairs = [arrived[:, head_width:]]
    distance = 1
    while distance < GROUP:
        pairs = pairs + [from_partner(pair, "fsdp", distance) for pair in pairs]
        distance *= 2
    known = jnp.concatenate(pairs, axis=0)

    def by_head(rows):
        return jnp.transpose(rows.reshape(rows.shape[0], local_heads, HEAD_DIM), (1, 0, 2))

    def by_head_t(rows):
        return jnp.transpose(rows.reshape(rows.shape[0], local_heads, HEAD_DIM), (1, 2, 0))

    scaled = arrived[:, :head_width] * jnp.asarray(0.125, bf16)
    queries, queries_t = by_head(scaled), by_head_t(scaled)
    key_rows, value_rows = known[:, :head_width], known[:, head_width:]
    keys, keys_t = by_head(key_rows), by_head_t(key_rows)
    values, values_t = by_head(value_rows), by_head_t(value_rows)
    extra = (local_heads, VALUE_ROWS - HEAD_DIM, values_t.shape[2])
    first = lax.broadcasted_iota(jnp.int32, extra, 1) == 0
    values_t = jnp.concatenate((values_t, first.astype(bf16)), axis=1)
    context_t, logsum = attend_forward(my_slopes, bases, queries_t, keys, values_t, count)

    sending = context_t.astype(bf16).reshape(head_width, groups, count)
    returned = [sending[:, 0]] + [from_sp(sending[:, p], p) for p in range(1, groups)]
    ordered = jnp.take(jnp.stack(returned), chunk, axis=0, mode="clip").reshape(width, count)
    context_rows = jnp.transpose(ordered)
    base = source.astype(f32)
    attended = product(context_rows, out_full)
    hidden, pull_one = jax.vjp(normalize, base + attended, gain_a, shift_a)
    hidden_low = hidden.astype(bf16)
    gate = product(hidden_low, gate_full)
    upward = product(hidden_low, up_full)
    active_full, pull_act = jax.vjp(geglu, gate, upward)
    active = active_full.astype(bf16)
    branch = product(active, down_full)
    result, pull_two = jax.vjp(normalize, hidden + branch, gain_b, shift_b)
    output = result.astype(bf16)[None]
    d_second, d_gain_b, d_shift_b = pull_two(cotangent[0].astype(f32))
    d_branch = d_second.astype(bf16)
    d_active = product_right(d_branch, down_full)
    d_gate, d_upward = pull_act(d_active)
    d_gate = d_gate.astype(bf16)
    d_upward = d_upward.astype(bf16)
    d_hidden = d_second + product_right(d_gate, gate_full) + product_right(d_upward, up_full)
    d_first, d_gain_a, d_shift_a = pull_one(d_hidden)
    d_attended = d_first.astype(bf16)
    d_context = product_right(d_attended, out_full).astype(bf16)

    d_parts = [
        lax.dynamic_slice_in_dim(d_context, (me ^ p) * head_width, head_width, axis=1)
        for p in range(groups)
    ]
    d_heads = [d_parts[0]] + [from_sp(d_parts[p], p) for p in range(1, groups)]
    d_heads = jnp.concatenate(d_heads, axis=0)

    grad_gate = product_left(hidden_low, d_gate)
    grad_up = product_left(hidden_low, d_upward)
    grad_down = product_left(active, d_branch)
    wide = []
    for p in range(groups):
        here = slice(p * hidden_part, (p + 1) * hidden_part)
        attended_part = lax.dynamic_slice_in_dim(
            d_attended, (me ^ p) * head_width, head_width, axis=1
        )
        out_part = product_left(context_rows, attended_part)
        wide.append((grad_gate[:, here], grad_up[:, here], grad_down[here], out_part))
    summed = [sum_to_quarter(parts) for parts in zip(*wide)]
    norm_grads = jnp.stack((d_gain_a, d_shift_a, d_gain_b, d_shift_b), axis=1)
    norm_share = lax.psum(
        lax.psum_scatter(norm_grads, "fsdp", scatter_dimension=0, tiled=True), "sp"
    )

    d_queries_t, d_keys, d_values = attend_backward(
        my_slopes,
        bases,
        queries_t,
        queries,
        by_head_t(d_heads),
        by_head(d_heads),
        context_t,
        logsum,
        keys,
        keys_t,
        values,
        count,
    )

    feed = scatter_rows(jnp.concatenate(summed[:3], axis=1))
    out_share = scatter_rows(summed[3])
    rows_here = w_gate.shape[0]

    def units(shared):
        split = shared.reshape(groups, rows_here, owners, piece_part)
        return jnp.transpose(split, (1, 2, 0, 3)).reshape(rows_here, hidden_units)

    def columns(shared):
        return jnp.transpose(shared, (1, 0, 2)).reshape(rows_here, width)

    pending = jnp.transpose(jnp.concatenate((d_keys, d_values), axis=0), (1, 0, 2))
    pending = pending.reshape(GROUP, seq_rows, 2 * head_width)
    while pending.shape[0] > 1:
        half = pending.shape[0] // 2
        leaving = pending[half:].astype(bf16)
        pending = pending[:half] + from_partner(leaving, "fsdp", half).astype(f32)
    d_queries = jnp.transpose(d_queries_t.reshape(head_width, seq_rows))
    d_all = jnp.concatenate((d_queries.astype(bf16), pending[0].astype(bf16)), axis=1)
    d_all = d_all.reshape(groups, count, 3 * head_width)
    d_rows = [d_all[0]] + [from_sp(d_all[p], p) for p in range(1, groups)]
    grad_threes = [product_left(source, rows) for rows in d_rows]
    d_tokens = d_first
    for rows, weight in zip(d_rows, threes):
        d_tokens = d_tokens + product_right(rows, weight)
    input_grad = d_tokens.astype(bf16)[None]
    three = scatter_rows(sum_to_quarter(grad_threes))
    return (
        output,
        input_grad,
        columns(three[:, :, :head_width]),
        columns(three[:, :, head_width : 2 * head_width]),
        columns(three[:, :, 2 * head_width :]),
        columns(out_share),
        norm_share[:, 0],
        norm_share[:, 1],
        units(feed[:, :, :hidden_part]),
        units(feed[:, :, hidden_part : 2 * hidden_part]),
        feed[:, :, 2 * hidden_part :].reshape(groups * piece_part, width),
        norm_share[:, 2],
        norm_share[:, 3],
    )


def solution(mesh):
    placed = (
        P("fsdp", "sp", None),
        P("fsdp", None),
        P("fsdp", None),
        P("fsdp", None),
        P("fsdp", None),
        P("fsdp"),
        P("fsdp"),
        P("fsdp", None),
        P("fsdp", None),
        P("fsdp", None),
        P("fsdp"),
        P("fsdp"),
        P(),
        P("fsdp", "sp", None),
    )
    return jax.shard_map(
        body,
        mesh=mesh,
        in_specs=placed,
        out_specs=(
            P("fsdp", "sp", None),
            P("fsdp", "sp", None),
            P("fsdp", None),
            P("fsdp", None),
            P("fsdp", None),
            P("fsdp", None),
            P("fsdp"),
            P("fsdp"),
            P("fsdp", None),
            P("fsdp", None),
            P("fsdp", None),
            P("fsdp"),
            P("fsdp"),
        ),
        check_vma=False,
    )
```

time: 1960 us -> 936 us (0.48)
  waiting for transfers between devices: 1130 us -> 346 us
  matrix products: 388 us -> 66.5 us
  Pallas kernels: 0 us -> 170 us
  local copies, waits for them, and re-layouts: 233 us -> 145 us
  other arithmetic: 99 us -> 57.1 us
  blocking collectives: 75 us -> 101 us
    reduce_scatter x4 -> x3, waiting for transfers between devices: 492 us -> 109 us  [scatter_rows(): lax.psum_scatter(quarter.astype(jnp.bfloat16), 'fsdp', scatter_dimension=...]
    unnamed x20 -> x9, waiting for transfers between devices: 232 us -> 34 us
    pallas_call x0 -> x2, Pallas kernels: none -> 170 us  [the longest x1 91.9 us: attend_backward(): pl.pallas_call(functools.partial(backward_kernel, block), grid=(heads, co...]
    dot_general x34 -> x8, matrix products: 148 us -> 15.5 us  [product_right(): lax.dot_general(left, right, (((1,), (1,)), ((), ())), preferred_element_...]
    dot_general x25 -> x8, matrix products: 144 us -> 25.1 us  [product(): return jnp.dot(left, right, preferred_element_type=jnp.float32)]
    all_gather x7 -> x4, waiting for transfers between devices: 124 us -> 10.3 us  [the longest x1 10.3 us: scatter_rows(): return lax.all_gather(low, 'sp', axis=0, tiled=False).astype(jnp.float32)]
    all_gather x0 -> x4, blocking collectives: none -> 95.6 us  [the longest x2 82.4 us: gather_rows(): return lax.all_gather(shard, 'fsdp', axis=0, tiled=True)]
    while x105 -> x0, local copies, waits for them, and re-layouts: 76.1 us -> none
  transfers between devices with their start and end apart: 22 -> 49, of which waited for: 16 -> 19; matrix products, arithmetic and copies ran while one was open for 15% -> 20% of each run, Pallas kernels for 0% -> 18%
where the time goes in v1:
time: 936 us; the launch traced here: 927 us
  waiting for transfers between devices  346 us (37%)
  Pallas kernels  170 us (18%)
  local copies, waits for them, and re-layouts  145 us (15%)
  blocking collectives  101 us (11%)
  matrix products  66.5 us (7%)
  other arithmetic  57.1 us (6%)
  starting transfers between devices  24.6 us (3%)
  between operations  15.8 us (2%)
    ppermute x41, waiting for transfers between devices, from_partner(): lax.ppermute(array, axis, [(i, i ^ distance) for i in range(lax.axis_size...  193 us
    reduce_scatter x3, waiting for transfers between devices, scatter_rows(): lax.psum_scatter(quarter.astype(jnp.bfloat16), 'fsdp', scatter_dimension=...  109 us
    pallas_call x1, Pallas kernels, attend_backward(): pl.pallas_call(functools.partial(backward_kernel, block), grid=(heads, co...  91.9 us
    all_gather x2, blocking collectives, gather_rows(): return lax.all_gather(shard, 'fsdp', axis=0, tiled=True)  82.4 us
    pallas_call x1, Pallas kernels, attend_forward(): pl.pallas_call(functools.partial(forward_kernel, block), grid=(heads, cou...  78.5 us
    unnamed x9, waiting for transfers between devices  34 us
    slice x4, local copies, waits for them, and re-layouts, body(): pending = pending[:half] + from_partner(leaving, 'fsdp', half).astype(f32)  32.1 us
    dot_general x11, matrix products, product_left(): lax.dot_general(left, right, (((0,), (0,)), ((), ())), preferred_element_...  25.9 us
  transfers between devices with their start and end apart: 49, of which 19 were waited for; matrix products, arithmetic and copies ran while one was open for 20% of the time, Pallas kernels for 18%

profile of v1, /device:TPU:0, one launch (start us, length us, event | category | flops | bytes accessed | tf_op | source)
XLA Modules:
  0.0 927.1 jit_solution(15052207514135318192)
XLA Ops:
  19.4 36.8 %all_gather.33 = bf16[768,576]{1,0:T(8,128)(2,1)S(1)} all-gather(bf16[96,576]{1,0:T(8,128)(2,1)S(1)} %pad_maximum_fusion.16), channel_id=1, replica_groups=mesh['sp'=4,'fsdp'=8] {'fsdp'}, dimensions={0}, use_global_device_ids=true | all-gather | bytes 995328 | tf_op jit(solution)/shard_map/all_gather | solution.py:227
  58.0 15.3 %collective-permute-done.2 = bf16[768,576]{0,1:T(8,128)(2,1)S(1)} collective-permute-done((bf16[768,576]{0,1:T(8,128)(2,1)S(1)}, bf16[768,576]{0,1:T(8,128)(2,1)S(1)}, u32[]{:S(2)}, u32[]{:S(2)}) %collective-permute-start.2) | collective-permute-done | bytes 884768 | tf_op jit(solution)/shard_map/ppermute | solution.py:21
  78.4 8.6 collective-permute-done.3
  87.0 8.7 collective-permute-done.5
  98.0 45.6 %all-gather.3 = bf16[8,96,4]{1,2,0:T(4,128)(2,1)S(1)} all-gather(bf16[1,96,4]{1,2,0:T(4,128)(2,1)S(1)} %maximum_bitcast_fusion.1), channel_id=1, replica_groups=mesh['sp'=4,'fsdp'=8] {'fsdp'}, dimensions={0}, use_global_device_ids=true | all-gather | bytes 6912 | tf_op jit(solution)/shard_map/all_gather | solution.py:227
  152.5 19.8 %collective-permute-done.16 = bf16[768,768]{1,0:T(8,128)(2,1)} collective-permute-done((bf16[768,768]{1,0:T(8,128)(2,1)}, bf16[768,768]{1,0:T(8,128)(2,1)}, u32[]{:S(2)}, u32[]{:S(2)}) %collective-permute-start.16) | collective-permute-done | bytes 1179680 | tf_op jit(solution)/shard_map/ppermute | solution.py:21
  183.5 24.6 %collective-permute-done.8 = bf16[1536,384]{0,1:T(8,128)(2,1)} collective-permute-done((bf16[1536,384]{0,1:T(8,128)(2,1)}, bf16[1536,384]{0,1:T(8,128)(2,1)}, u32[]{:S(2)}, u32[]{:S(2)}) %collective-permute-start.8) | collective-permute-done | bytes 1179680 | tf_op jit(solution)/shard_map/ppermute | solution.py:21
  213.4 5.7 copy.206.k_ref
  223.0 78.5 %shard_map.237 = (f32[3,64,1536]{2,1,0:T(8,128)S(1)}, f32[3,1,1536]{2,1,0:T(1,128)S(1)}) custom-call(f32[3]{0:T(128)S(1)} %dynamic_slice.46.slopes_ref, f32[16]{0:T(128)S(1)} %convert_element_type.201.bases_ref, bf16[3,64,1536]{2,1,0:T(8,128)(2,1)S(1)} %bitcast.181, bf16[3,6144,64]{2,1,0:T(8,128)(2,1)} %copy.206.k_ref, ...), custom_call_target="tpu_custom_call" | custom-call | flops 28991029248 | bytes 18874368 | tf_op jit(solution)/shard_map/pallas_call | solution.py:167
  314.6 5.7 copy.217
  333.6 16.0 %multiply_convert_fusion.1 = (bf16[384,3072]{1,0:T(8,128)(2,1)S(1)}, f32[384,3072]{1,0:T(8,128)S(1)}, f32[384,3072]{1,0:T(8,128)}) fusion(f32[384,3072]{1,0:T(8,128)S(1)} %fusion.39, bf16[384,768]{1,0:T(8,128)(2,1)S(1)} %fusion.36, bf16[768,768]{1,0:T(8,128)(2,1)S(1)} %get-tuple-element.55, bf16[768,768]{1,0:T(8,128)(2,1)S(1)} %get-tuple-element.53, ...), kind=kOutput, calls=%fused_computation.11 | convolution fusion | flops 1908670464 | bytes 21823488 | tf_op jit(solution)/shard_map/dot_general | solution.py:40
  406.0 91.9 %shard_map.238 = (f32[3,64,1536]{2,1,0:T(8,128)S(1)}, f32[3,6144,64]{2,1,0:T(8,128)}, f32[3,6144,64]{2,1,0:T(8,128)}) custom-call(f32[3]{0:T(128)S(1)} %dynamic_slice.46.slopes_ref, f32[16]{0:T(128)S(1)} %convert_element_type.201.bases_ref, bf16[3,64,1536]{2,1,0:T(8,128)(2,1)S(1)} %bitcast.182, bf16[3,1536,64]{2,1,0:T(8,128)(2,1)S(1)} %bitcast.185, ...), custom_call_target="tpu_custom_call" | custom-call | flops 72477573120 | bytes 37748736 | tf_op jit(solution)/shard_map/pallas_call | solution.py:196
  510.7 10.8 %maximum_bitcast_fusion = f32[6144,6,64]{2,0,1:T(8,128)} fusion(f32[3,6144,64]{2,1,0:T(8,128)} %get-tuple-element.22, f32[3,6144,64]{2,1,0:T(8,128)S(1)} %copy-done.11), kind=kLoop, calls=%fused_computation.1 | loop fusion | flops 2359296 | bytes 18874368 | tf_op jit(solution)/shard_map/transpose | solution.py:410
  521.6 6.4 slice.329
  535.7 5.8 copy.222
  544.7 11.0 %collective-permute-done.37 = bf16[768,768]{1,0:T(8,128)(2,1)} collective-permute-done((bf16[768,768]{1,0:T(8,128)(2,1)}, bf16[768,768]{1,0:T(8,128)(2,1)}, u32[]{:S(2)}, u32[]{:S(2)}) %collective-permute-start.37) | collective-permute-done | bytes 1179680 | tf_op jit(solution)/shard_map/ppermute | solution.py:21
  558.4 22.1 %collective-permute-done.40 = bf16[768,768]{1,0:T(8,128)(2,1)} collective-permute-done((bf16[768,768]{1,0:T(8,128)(2,1)}, bf16[768,768]{1,0:T(8,128)(2,1)}, u32[]{:S(2)}, u32[]{:S(2)}) %collective-permute-start.40) | collective-permute-done | bytes 1179680 | tf_op jit(solution)/shard_map/ppermute | solution.py:21
  585.1 7.9 slice.237
  593.0 8.8 copy.220
  601.8 7.2 slice.187
  609.1 8.2 copy.223
  623.3 32.6 %collective-permute-done.22 = bf16[1,1536,384]{2,1,0:T(8,128)(2,1)} collective-permute-done((bf16[1,1536,384]{2,1,0:T(8,128)(2,1)S(1)}, bf16[1,1536,384]{2,1,0:T(8,128)(2,1)}, u32[]{:S(2)}, u32[]{:S(2)}) %collective-permute-start.22) | collective-permute-done | bytes 1179680 | tf_op jit(solution)/shard_map/ppermute | solution.py:21
  660.4 11.7 %collective-permute-done.25 = bf16[384,576]{1,0:T(8,128)(2,1)S(1)} collective-permute-done((bf16[384,576]{1,0:T(8,128)(2,1)S(1)}, bf16[384,576]{1,0:T(8,128)(2,1)S(1)}, u32[]{:S(2)}, u32[]{:S(2)}) %collective-permute-start.25) | collective-permute-done | bytes 442400 | tf_op jit(solution)/shard_map/ppermute | solution.py:21
  679.0 9.9 %collective-permute-done.24 = bf16[384,576]{1,0:T(8,128)(2,1)S(1)} collective-permute-done((bf16[384,576]{1,0:T(8,128)(2,1)S(1)}, bf16[384,576]{1,0:T(8,128)(2,1)S(1)}, u32[]{:S(2)}, u32[]{:S(2)}) %collective-permute-start.24) | collective-permute-done | bytes 442400 | tf_op jit(solution)/shard_map/ppermute | solution.py:21
  697.4 16.4 %collective-permute-done.28 = bf16[768,576]{0,1:T(8,128)(2,1)} collective-permute-done((bf16[768,576]{0,1:T(8,128)(2,1)}, bf16[768,576]{0,1:T(8,128)(2,1)}, u32[]{:S(2)}, u32[]{:S(2)}) %collective-permute-start.28) | collective-permute-done | bytes 884768 | tf_op jit(solution)/shard_map/ppermute | solution.py:21
  720.0 33.2 %reduce-scatter.17.cloned.1.call-done = f32[96,4]{1,0:T(8,128)} async-done(((f32[768,4]{1,0:T(8,128)}), f32[96,4]{1,0:T(8,128)}) %reduce-scatter.17.cloned.1.call-update) | async-done | bytes 1552
  754.0 5.6 psum.7
  760.2 56.5 %reduce-scatter.15.cloned.1.call-done = bf16[96,192]{1,0:T(8,128)(2,1)} async-done(((bf16[768,192]{1,0:T(8,128)(2,1)}), bf16[96,192]{1,0:T(8,128)(2,1)}) %reduce-scatter.15.cloned.1.call-update) | async-done | bytes 36880 | tf_op jit(solution)/shard_map/reduce_scatter | solution.py:243
  816.7 6.1 all-gather.1
  830.5 52.6 %reduce-scatter.13.cloned.1.call-done = bf16[96,576]{1,0:T(8,128)(2,1)} async-done(((bf16[768,576]{1,0:T(8,128)(2,1)}), bf16[96,576]{1,0:T(8,128)(2,1)}) %reduce-scatter.13.cloned.1.call-update) | async-done | bytes 110608 | tf_op jit(solution)/shard_map/reduce_scatter | solution.py:243
  883.1 7.2 all-gather
  894.2 10.3 %all-gather.15.cloned.1.call-done = bf16[384,2304]{1,0:T(8,128)(2,1)} async-done(((bf16[96,2304]{1,0:T(8,128)(2,1)}), bf16[384,2304]{1,0:T(8,128)(2,1)}) %all-gather.15.cloned.1.call-update) | async-done | bytes 1769488 | tf_op jit(solution)/shard_map/all_gather | solution.py:246
  (362 shorter events, 223.7 us)
Async XLA Ops:
  7.2 136.5 %all-gather.13.cloned.1.call-start = ((), (), s32[]{:S(2)}) async-start(), calls=%async_computation.6 | async-start | bytes 1327104 | tf_op jit(solution)/shard_map/all_gather | solution.py:227
  8.9 168.2 %all-gather.11.cloned.1.call-start = ((), (), s32[]{:S(2)}) async-start(), calls=%async_computation.5 | async-start | bytes 2654208 | tf_op jit(solution)/shard_map/all_gather | solution.py:227
  17.2 304.0 %all-gather.9.cloned.1.call-start = ((), (), s32[]{:S(2)}) async-start(), calls=%async_computation.4 | async-start | bytes 1327104 | tf_op jit(solution)/shard_map/all_gather | solution.py:227
  76.6 19.2 %collective-permute-start.5 = (bf16[384,576]{0,1:T(8,128)(2,1)S(1)}, bf16[384,576]{0,1:T(8,128)(2,1)S(1)}, u32[]{:S(2)}, u32[]{:S(2)}) collective-permute-start(bf16[384,576]{0,1:T(8,128)(2,1)S(1)} %fusion.32), channel_id=1, source_target_pairs={{0,24},{8,16},{16,8},{24,0},{1,25},{9,17},{17,9},{25,1},{2,26},{10... | collective-permute-start | bytes 1327112 | tf_op jit(solution)/shard_map/ppermute | solution.py:21
  96.5 48.7 %collective-permute-start.6 = (bf16[1536,384]{0,1:T(8,128)(2,1)S(1)}, bf16[1536,384]{0,1:T(8,128)(2,1)}, u32[]{:S(2)}, u32[]{:S(2)}) collective-permute-start(bf16[1536,384]{0,1:T(8,128)(2,1)S(1)} %pad_maximum_fusion.5), channel_id=1, source_target_pairs={{0,1},{1,0},{2,3},{3,2},{4,5},{5,4},{6,7},{7,6},{8,9},{9,8},{10,11... | collective-permute-start | bytes 3538952 | tf_op jit(solution)/shard_map/ppermute | solution.py:21
  97.9 621.4 %reduce-scatter.11.cloned.1.call-start = ((), (), s32[]{:S(2)}) async-start(), calls=%async_computation.7 | async-start | bytes 3981312 | tf_op jit(solution)/shard_map/reduce_scatter | solution.py:243
  143.7 28.7 %collective-permute-start.15 = (bf16[768,768]{1,0:T(8,128)(2,1)}, bf16[768,768]{1,0:T(8,128)(2,1)}, u32[]{:S(2)}, u32[]{:S(2)}) collective-permute-start(bf16[768,768]{1,0:T(8,128)(2,1)} %all-gather.13.cloned.1.call-done), channel_id=1, source_target_pairs={{0,8},{8,0},{16,24},{24,16},{1,9},{9,1},{17,25},{25,17},{2,10},{10... | collective-permute-start | bytes 3538952 | tf_op jit(solution)/shard_map/ppermute | solution.py:21
  143.7 28.7 %collective-permute-start.16 = (bf16[768,768]{1,0:T(8,128)(2,1)}, bf16[768,768]{1,0:T(8,128)(2,1)}, u32[]{:S(2)}, u32[]{:S(2)}) collective-permute-start(bf16[768,768]{1,0:T(8,128)(2,1)} %all-gather.13.cloned.1.call-done), channel_id=1, source_target_pairs={{0,16},{8,24},{16,0},{24,8},{1,17},{9,25},{17,1},{25,9},{2,18},{10... | collective-permute-start | bytes 3538952 | tf_op jit(solution)/shard_map/ppermute | solution.py:21
  145.1 38.4 %collective-permute-start.7 = (bf16[1536,384]{0,1:T(8,128)(2,1)S(1)}, bf16[1536,384]{0,1:T(8,128)(2,1)}, u32[]{:S(2)}, u32[]{:S(2)}) collective-permute-start(bf16[1536,384]{0,1:T(8,128)(2,1)S(1)} %pad_maximum_fusion.5), channel_id=1, source_target_pairs={{0,2},{1,3},{2,0},{3,1},{4,6},{5,7},{6,4},{7,5},{8,10},{9,11},{10,... | collective-permute-start | bytes 3538952 | tf_op jit(solution)/shard_map/ppermute | solution.py:21
  145.2 62.9 %collective-permute-start.8 = (bf16[1536,384]{0,1:T(8,128)(2,1)}, bf16[1536,384]{0,1:T(8,128)(2,1)}, u32[]{:S(2)}, u32[]{:S(2)}) collective-permute-start(bf16[1536,384]{0,1:T(8,128)(2,1)} %collective-permute-done.6), channel_id=1, source_target_pairs={{0,2},{1,3},{2,0},{3,1},{4,6},{5,7},{6,4},{7,5},{8,10},{9,11},{10,... | collective-permute-start | bytes 3538952 | tf_op jit(solution)/shard_map/ppermute | solution.py:21
  172.4 136.6 %collective-permute-start.17 = (bf16[768,768]{1,0:T(8,128)(2,1)}, bf16[768,768]{1,0:T(8,128)(2,1)}, u32[]{:S(2)}, u32[]{:S(2)}) collective-permute-start(bf16[768,768]{1,0:T(8,128)(2,1)} %collective-permute-done.16), channel_id=1, source_target_pairs={{0,8},{8,0},{16,24},{24,16},{1,9},{9,1},{17,25},{25,17},{2,10},{10... | collective-permute-start | bytes 3538952 | tf_op jit(solution)/shard_map/ppermute | solution.py:21
  177.1 133.2 %collective-permute-start.13 = (bf16[768,1536]{1,0:T(8,128)(2,1)}, bf16[768,1536]{1,0:T(8,128)(2,1)}, u32[]{:S(2)}, u32[]{:S(2)}) collective-permute-start(bf16[768,1536]{1,0:T(8,128)(2,1)} %all-gather.11.cloned.1.call-done), channel_id=1, source_target_pairs={{0,16},{8,24},{16,0},{24,8},{1,17},{9,25},{17,1},{25,9},{2,18},{10... | collective-permute-start | bytes 7077896 | tf_op jit(solution)/shard_map/ppermute | solution.py:21
  178.6 147.4 %collective-permute-start.12 = (bf16[768,1536]{1,0:T(8,128)(2,1)}, bf16[768,1536]{1,0:T(8,128)(2,1)}, u32[]{:S(2)}, u32[]{:S(2)}) collective-permute-start(bf16[768,1536]{1,0:T(8,128)(2,1)} %all-gather.11.cloned.1.call-done), channel_id=1, source_target_pairs={{0,8},{8,0},{16,24},{24,16},{1,9},{9,1},{17,25},{25,17},{2,10},{10... | collective-permute-start | bytes 7077896 | tf_op jit(solution)/shard_map/ppermute | solution.py:21
  383.4 114.5 %collective-permute-start.33 = (bf16[768,768]{1,0:T(8,128)(2,1)}, bf16[768,768]{1,0:T(8,128)(2,1)}, u32[]{:S(2)}, u32[]{:S(2)}) collective-permute-start(bf16[768,768]{1,0:T(8,128)(2,1)} %get-tuple-element.41), channel_id=1, source_target_pairs={{0,8},{8,0},{16,24},{24,16},{1,9},{9,1},{17,25},{25,17},{2,10},{10... | collective-permute-start | bytes 3538952 | tf_op jit(solution)/shard_map/ppermute | solution.py:21
  383.6 126.3 %collective-permute-start.32 = (bf16[768,768]{1,0:T(8,128)(2,1)}, bf16[768,768]{1,0:T(8,128)(2,1)}, u32[]{:S(2)}, u32[]{:S(2)}) collective-permute-start(bf16[768,768]{1,0:T(8,128)(2,1)} %get-tuple-element.40), channel_id=1, source_target_pairs={{0,8},{8,0},{16,24},{24,16},{1,9},{9,1},{17,25},{25,17},{2,10},{10... | collective-permute-start | bytes 3538952 | tf_op jit(solution)/shard_map/ppermute | solution.py:21
  395.5 105.8 %collective-permute-start.36 = (bf16[768,768]{1,0:T(8,128)(2,1)}, bf16[768,768]{1,0:T(8,128)(2,1)}, u32[]{:S(2)}, u32[]{:S(2)}) collective-permute-start(bf16[768,768]{1,0:T(8,128)(2,1)} %get-tuple-element.43), channel_id=1, source_target_pairs={{0,8},{8,0},{16,24},{24,16},{1,9},{9,1},{17,25},{25,17},{2,10},{10... | collective-permute-start | bytes 3538952 | tf_op jit(solution)/shard_map/ppermute | solution.py:21
  400.0 144.6 %collective-permute-start.35 = (bf16[768,768]{1,0:T(8,128)(2,1)}, bf16[768,768]{1,0:T(8,128)(2,1)}, u32[]{:S(2)}, u32[]{:S(2)}) collective-permute-start(bf16[768,768]{1,0:T(8,128)(2,1)} %get-tuple-element.42), channel_id=1, source_target_pairs={{0,8},{8,0},{16,24},{24,16},{1,9},{9,1},{17,25},{25,17},{2,10},{10... | collective-permute-start | bytes 3538952 | tf_op jit(solution)/shard_map/ppermute | solution.py:21
  403.0 102.2 %collective-permute-start.39 = (bf16[768,768]{1,0:T(8,128)(2,1)}, bf16[768,768]{1,0:T(8,128)(2,1)}, u32[]{:S(2)}, u32[]{:S(2)}) collective-permute-start(bf16[768,768]{1,0:T(8,128)(2,1)} %get-tuple-element.45), channel_id=1, source_target_pairs={{0,8},{8,0},{16,24},{24,16},{1,9},{9,1},{17,25},{25,17},{2,10},{10... | collective-permute-start | bytes 3538952 | tf_op jit(solution)/shard_map/ppermute | solution.py:21
  497.9 60.5 %collective-permute-start.38 = (bf16[768,768]{1,0:T(8,128)(2,1)}, bf16[768,768]{1,0:T(8,128)(2,1)}, u32[]{:S(2)}, u32[]{:S(2)}) collective-permute-start(bf16[768,768]{1,0:T(8,128)(2,1)} %get-tuple-element.44), channel_id=1, source_target_pairs={{0,8},{8,0},{16,24},{24,16},{1,9},{9,1},{17,25},{25,17},{2,10},{10... | collective-permute-start | bytes 3538952 | tf_op jit(solution)/shard_map/ppermute | solution.py:21
  501.3 40.3 %collective-permute-start.34 = (bf16[768,768]{1,0:T(8,128)(2,1)}, bf16[768,768]{1,0:T(8,128)(2,1)}, u32[]{:S(2)}, u32[]{:S(2)}) collective-permute-start(bf16[768,768]{1,0:T(8,128)(2,1)} %fusion.12), channel_id=1, source_target_pairs={{0,16},{8,24},{16,0},{24,8},{1,17},{9,25},{17,1},{25,9},{2,18},{10... | collective-permute-start | bytes 3538952 | tf_op jit(solution)/shard_map/ppermute | solution.py:21
  505.2 50.4 %collective-permute-start.37 = (bf16[768,768]{1,0:T(8,128)(2,1)}, bf16[768,768]{1,0:T(8,128)(2,1)}, u32[]{:S(2)}, u32[]{:S(2)}) collective-permute-start(bf16[768,768]{1,0:T(8,128)(2,1)} %fusion.9), channel_id=1, source_target_pairs={{0,16},{8,24},{16,0},{24,8},{1,17},{9,25},{17,1},{25,9},{2,18},{10... | collective-permute-start | bytes 3538952 | tf_op jit(solution)/shard_map/ppermute | solution.py:21
  510.0 70.5 %collective-permute-start.40 = (bf16[768,768]{1,0:T(8,128)(2,1)}, bf16[768,768]{1,0:T(8,128)(2,1)}, u32[]{:S(2)}, u32[]{:S(2)}) collective-permute-start(bf16[768,768]{1,0:T(8,128)(2,1)} %fusion.6), channel_id=1, source_target_pairs={{0,16},{8,24},{16,0},{24,8},{1,17},{9,25},{17,1},{25,9},{2,18},{10... | collective-permute-start | bytes 3538952 | tf_op jit(solution)/shard_map/ppermute | solution.py:21
  541.6 75.7 %collective-permute-start.21 = (bf16[2,1536,384]{2,1,0:T(8,128)(2,1)S(1)}, bf16[2,1536,384]{2,1,0:T(8,128)(2,1)}, u32[]{:S(2)}, u32[]{:S(2)}) collective-permute-start(bf16[2,1536,384]{2,1,0:T(8,128)(2,1)S(1)} %copy.222), channel_id=1, source_target_pairs={{0,2},{1,3},{2,0},{3,1},{4,6},{5,7},{6,4},{7,5},{8,10},{9,11},{10,... | collective-permute-start | bytes 7077896 | tf_op jit(solution)/shard_map/ppermute | solution.py:21
  585.1 168.1 %reduce-scatter.17.cloned.1.call-start = ((), (), s32[]{:S(2)}) async-start(), calls=%async_computation.11 | async-start | bytes 442368
  620.9 34.9 %collective-permute-start.22 = (bf16[1,1536,384]{2,1,0:T(8,128)(2,1)S(1)}, bf16[1,1536,384]{2,1,0:T(8,128)(2,1)}, u32[]{:S(2)}, u32[]{:S(2)}) collective-permute-start(bf16[1,1536,384]{2,1,0:T(8,128)(2,1)S(1)} %slice.330), channel_id=1, source_target_pairs={{0,1},{1,0},{2,3},{3,2},{4,5},{5,4},{6,7},{7,6},{8,9},{9,8},{10,11... | collective-permute-start | bytes 3538952 | tf_op jit(solution)/shard_map/ppermute | solution.py:21
  674.8 20.2 %collective-permute-start.29 = (bf16[768,192]{0,1:T(8,128)(2,1)}, bf16[768,192]{0,1:T(8,128)(2,1)}, u32[]{:S(2)}, u32[]{:S(2)}) collective-permute-start(bf16[768,192]{0,1:T(8,128)(2,1)} %convolution_convert_fusion.8), channel_id=1, source_target_pairs={{0,8},{8,0},{16,24},{24,16},{1,9},{9,1},{17,25},{25,17},{2,10},{10... | collective-permute-start | bytes 884744 | tf_op jit(solution)/shard_map/ppermute | solution.py:21
  676.6 18.7 %collective-permute-start.31 = (bf16[768,192]{0,1:T(8,128)(2,1)S(1)}, bf16[768,192]{0,1:T(8,128)(2,1)}, u32[]{:S(2)}, u32[]{:S(2)}) collective-permute-start(bf16[768,192]{0,1:T(8,128)(2,1)S(1)} %add_convert_fusion.5), channel_id=1, source_target_pairs={{0,16},{8,24},{16,0},{24,8},{1,17},{9,25},{17,1},{25,9},{2,18},{10... | collective-permute-start | bytes 884744 | tf_op jit(solution)/shard_map/ppermute | solution.py:21
  679.0 18.5 %collective-permute-start.26 = (bf16[768,576]{0,1:T(8,128)(2,1)}, bf16[768,576]{0,1:T(8,128)(2,1)}, u32[]{:S(2)}, u32[]{:S(2)}) collective-permute-start(bf16[768,576]{0,1:T(8,128)(2,1)} %fusion.26), channel_id=1, source_target_pairs={{0,8},{8,0},{16,24},{24,16},{1,9},{9,1},{17,25},{25,17},{2,10},{10... | collective-permute-start | bytes 2654216 | tf_op jit(solution)/shard_map/ppermute | solution.py:21
  691.2 22.6 %collective-permute-start.28 = (bf16[768,576]{0,1:T(8,128)(2,1)}, bf16[768,576]{0,1:T(8,128)(2,1)}, u32[]{:S(2)}, u32[]{:S(2)}) collective-permute-start(bf16[768,576]{0,1:T(8,128)(2,1)} %fusion.16), channel_id=1, source_target_pairs={{0,16},{8,24},{16,0},{24,8},{1,17},{9,25},{17,1},{25,9},{2,18},{10... | collective-permute-start | bytes 2654216 | tf_op jit(solution)/shard_map/ppermute | solution.py:21
  693.4 123.3 %reduce-scatter.15.cloned.1.call-start = ((), (), s32[]{:S(2)}) async-start(), calls=%async_computation.10 | async-start | bytes 442368 | tf_op jit(solution)/shard_map/reduce_scatter | solution.py:243
  697.4 185.8 %reduce-scatter.13.cloned.1.call-start = ((), (), s32[]{:S(2)}) async-start(), calls=%async_computation.9 | async-start | bytes 1105920 | tf_op jit(solution)/shard_map/reduce_scatter | solution.py:243
  719.2 185.3 %all-gather.15.cloned.1.call-start = ((), (), s32[]{:S(2)}) async-start(), calls=%async_computation.8 | async-start | bytes 2211840 | tf_op jit(solution)/shard_map/all_gather | solution.py:246
  (82 other events, 845.3 us)
Sparse Core Ops, SparseCore 0:
  10.8 51.2 all-gather.12
  64.8 59.3 all-gather.10
  126.4 43.8 all-gather.8
  585.2 87.5 reduce-scatter.10
  693.6 59.5 reduce-scatter.16
  756.3 60.3 reduce-scatter.14
  820.6 62.4 reduce-scatter.12
  884.7 19.7 all-gather.14

commit v2 on v1

--- a/solution.py
+++ b/solution.py
@@ -92,6 +92,7 @@
 
 
 def backward_kernel(
+    head,
     block,
     slopes_ref,
     bases_ref,
@@ -105,12 +106,12 @@
     kt_ref,
     v_ref,
     dq_ref,
+    pair_ref,
     dk_ref,
     dv_ref,
     tile_ref,
 ):
-    head = pl.program_id(0)
-    place = pl.program_id(1)
+    place = pl.program_id(0)
     slope = slopes_ref[head]
 
     @pl.when(place == 0)
@@ -132,10 +133,10 @@
         probs = jnp.exp(raw - jnp.abs(tile_ref[...] + shift) - logsum)
         d_probs = jnp.dot(v_ref[0, rows, :], grads_t, preferred_element_type=jnp.float32)
         d_scores = (probs * (d_probs - means)).astype(jnp.bfloat16)
-        dv_ref[0, rows, :] += jnp.dot(
+        dv_ref[rows, :] += jnp.dot(
             probs.astype(jnp.bfloat16), g_ref[0], preferred_element_type=jnp.float32
         )
-        dk_ref[0, rows, :] += jnp.dot(d_scores, q_ref[0], preferred_element_type=jnp.float32)
+        dk_ref[rows, :] += jnp.dot(d_scores, q_ref[0], preferred_element_type=jnp.float32)
         return total + jnp.dot(kt_ref[0, :, rows], d_scores, preferred_element_type=jnp.float32)
 
     chunks = k_ref.shape[1] // block
@@ -143,6 +144,10 @@
     total = lax.fori_loop(0, chunks, step, total, unroll=2)
     dq_ref[0] = total * 0.125
 
+    @pl.when(place == pl.num_programs(0) - 1)
+    def _():
+        pair_ref[...] = jnp.concatenate((dk_ref[...], dv_ref[...]), axis=1).astype(jnp.bfloat16)
+
 
 def scalars():
     return pl.BlockSpec(memory_space=pltpu.SMEM)
@@ -150,10 +155,6 @@
 
 def across(rows, block):
     return pl.BlockSpec((1, rows, block), lambda h, i: (h, 0, i))
-
-
-def down(block):
-    return pl.BlockSpec((1, block, HEAD_DIM), lambda h, i: (h, i, 0))
 
 
 def whole(rows, columns):
@@ -188,37 +189,51 @@
 
 
 def attend_backward(
-    slopes, bases, queries_t, queries, grads_t, grads, context_t, logsum, keys, keys_t, values, block
+    head, slopes, bases, queries_t, queries, grads_t, grads, context_t, logsum, keys, keys_t, values, block
 ):
     heads, width, count = queries_t.shape
     length = keys.shape[1]
-    work = heads * count * length
+    work = count * length
+
+    def across_one(rows):
+        return pl.BlockSpec((1, rows, block), lambda i: (head, 0, i))
+
+    def whole_one(rows, columns):
+        return pl.BlockSpec((1, rows, columns), lambda i: (head, 0, 0))
+
+    down_one = pl.BlockSpec((1, block, width), lambda i: (head, i, 0))
     return pl.pallas_call(
-        functools.partial(backward_kernel, block),
-        grid=(heads, count // block),
+        functools.partial(backward_kernel, head, block),
+        grid=(count // block,),
         in_specs=[
             scalars(),
             scalars(),
-            across(width, block),
-            down(block),
-            across(width, block),
-            down(block),
-            across(width, block),
-            across(1, block),
-            whole(length, width),
-            whole(width, length),
-            whole(length, width),
+            across_one(width),
+            down_one,
+            across_one(width),
+            down_one,
+            across_one(width),
+            across_one(1),
+            whole_one(length, width),
+            whole_one(width, length),
+            whole_one(length, width),
         ],
-        out_specs=[across(width, block), whole(length, width), whole(length, width)],
+        out_specs=[
+            pl.BlockSpec((1, width, block), lambda i: (0, 0, i)),
+            pl.BlockSpec((length, 2 * width), lambda i: (0, 0)),
+        ],
         out_shape=[
-            jax.ShapeDtypeStruct((heads, width, count), jnp.float32),
-            jax.ShapeDtypeStruct((heads, length, width), jnp.float32),
-            jax.ShapeDtypeStruct((heads, length, width), jnp.float32),
+            jax.ShapeDtypeStruct((1, width, count), jnp.float32),
+            jax.ShapeDtypeStruct((length, 2 * width), jnp.bfloat16),
         ],
-        scratch_shapes=[pltpu.VMEM((block, block), jnp.float32)],
+        scratch_shapes=[
+            pltpu.VMEM((length, width), jnp.float32),
+            pltpu.VMEM((length, width), jnp.float32),
+            pltpu.VMEM((block, block), jnp.float32),
+        ],
         compiler_params=pltpu.CompilerParams(vmem_limit_bytes=VMEM_BYTES),
         cost_estimate=pl.CostEstimate(
-            flops=40 * work * width, bytes_accessed=32 * heads * length * width, transcendentals=work
+            flops=40 * work * width, bytes_accessed=32 * length * width, transcendentals=work
         ),
     )(slopes, bases, queries_t, queries, grads_t, grads, context_t, logsum, keys, keys_t, values)
 
@@ -232,18 +247,34 @@
     return (mine, from_sp(mine, 1), opposite, from_sp(opposite, 1))
 
 
-def sum_to_quarter(parts):
-    low = [part.astype(jnp.bfloat16) for part in parts]
-    near = parts[0] + from_sp(low[1], 1).astype(jnp.float32)
-    far = parts[2] + from_sp(low[3], 1).astype(jnp.float32)
-    return near + from_sp(far.astype(jnp.bfloat16), 2).astype(jnp.float32)
-
-
-def scatter_rows(quarter):
-    low = lax.psum_scatter(
-        quarter.astype(jnp.bfloat16), "fsdp", scatter_dimension=0, tiled=True
-    )
-    return lax.all_gather(low, "sp", axis=0, tiled=False).astype(jnp.float32)
+def sum_near(low):
+    near = low[0].astype(jnp.float32) + from_sp(low[1], 1).astype(jnp.float32)
+    far = low[2].astype(jnp.float32) + from_sp(low[3], 1).astype(jnp.float32)
+    return near, far.astype(jnp.bfloat16)
+
+
+def sum_far(near, far):
+    return (near + from_sp(far, 2).astype(jnp.float32)).astype(jnp.bfloat16)
+
+
+def halve_rows(rows):
+    distance = rows.shape[0] // 2
+    flips = []
+    step = 1
+    while step <= distance:
+        flips.append(step)
+        step *= 2
+    kept = [rows[i] for i in range(rows.shape[0])]
+    for flip in flips:
+        leaving = jnp.concatenate(kept[1::2], axis=0).astype(jnp.bfloat16)
+        landed = from_partner(leaving, "fsdp", flip).astype(jnp.float32)
+        landed = landed.reshape((len(kept) // 2,) + rows.shape[1:])
+        kept = [kept[2 * i] + landed[i] for i in range(len(kept) // 2)]
+    return kept[0]
+
+
+def share_rows(quarter):
+    return lax.all_gather(quarter.astype(jnp.bfloat16), "sp", axis=0, tiled=False).astype(jnp.float32)
 
 
 def body(
@@ -290,14 +321,15 @@
     vectors = jnp.stack((gain_one, shift_one, gain_two, shift_two), axis=1)
     my_down = lax.dynamic_slice_in_dim(w_down, me * piece_part, piece_part, axis=0)
     w_pairs = gather_rows(jnp.concatenate((my_units(w_gate), my_units(w_up)), axis=1))
-    w_rest = gather_rows(my_down)
-    out_full = gather_rows(w_out)
-    vectors_full = gather_rows(vectors).astype(f32)
+    vectors = jnp.pad(vectors, ((0, 0), (0, 128 - vectors.shape[1])))
+    w_rest = gather_rows(jnp.concatenate((my_down, w_out, vectors), axis=1))
+    out_full = w_rest[:, width : 2 * width]
+    vectors_full = w_rest[:, 2 * width :].astype(f32)
     gain_a, shift_a, gain_b, shift_b = [vectors_full[:, i] for i in range(4)]
     pair_parts = four_from_sp(w_pairs)
     gate_full = jnp.concatenate([part[:, :hidden_part] for part in pair_parts], axis=1)
     up_full = jnp.concatenate([part[:, hidden_part:] for part in pair_parts], axis=1)
-    down_full = jnp.concatenate(four_from_sp(w_rest), axis=0)
+    down_full = jnp.concatenate(four_from_sp(w_rest[:, :width]), axis=0)
 
     projected = [product(source, weight).astype(bf16) for weight in threes]
     arrived = [projected[0]] + [from_sp(projected[p], p) for p in range(1, groups)]
@@ -367,6 +399,7 @@
     grad_gate = product_left(hidden_low, d_gate)
     grad_up = product_left(hidden_low, d_upward)
     grad_down = product_left(active, d_branch)
+    norm_grads = jnp.stack((d_gain_a, d_shift_a, d_gain_b, d_shift_b), axis=1)
     wide = []
     for p in range(groups):
         here = slice(p * hidden_part, (p + 1) * hidden_part)
@@ -374,30 +407,46 @@
             d_attended, (me ^ p) * head_width, head_width, axis=1
         )
         out_part = product_left(context_rows, attended_part)
-        wide.append((grad_gate[:, here], grad_up[:, here], grad_down[here], out_part))
-    summed = [sum_to_quarter(parts) for parts in zip(*wide)]
-    norm_grads = jnp.stack((d_gain_a, d_shift_a, d_gain_b, d_shift_b), axis=1)
-    norm_share = lax.psum(
-        lax.psum_scatter(norm_grads, "fsdp", scatter_dimension=0, tiled=True), "sp"
-    )
-
-    d_queries_t, d_keys, d_values = attend_backward(
-        my_slopes,
-        bases,
-        queries_t,
-        queries,
-        by_head_t(d_heads),
-        by_head(d_heads),
-        context_t,
-        logsum,
-        keys,
-        keys_t,
-        values,
-        count,
-    )
-
-    feed = scatter_rows(jnp.concatenate(summed[:3], axis=1))
-    out_share = scatter_rows(summed[3])
+        norm_part = lax.dynamic_slice_in_dim(norm_grads, me ^ p, 1, axis=1)
+        side = jnp.concatenate((out_part, jnp.pad(norm_part, ((0, 0), (0, 63)))), axis=1)
+        parts = (grad_gate[:, here], grad_up[:, here], grad_down[here], side)
+        wide.append(jnp.concatenate([part.astype(bf16) for part in parts], axis=1))
+    d_heads_t, d_heads_n = by_head_t(d_heads), by_head(d_heads)
+    d_heads_t, d_heads_n, wide = lax.optimization_barrier((d_heads_t, d_heads_n, wide))
+    d_head_queries, d_head_pairs = [], []
+    held = None
+    for head in range(local_heads):
+        if head == 1:
+            near, far = sum_near(wide)
+            d_heads_t, near, far = lax.optimization_barrier((d_heads_t, near, far))
+        elif head == 2:
+            quarter = sum_far(near, far)
+            d_heads_t, quarter = lax.optimization_barrier((d_heads_t, quarter))
+        if head:
+            d_heads_t, held = lax.optimization_barrier((d_heads_t, held))
+            d_head_queries[-1] = held
+        held, pair = attend_backward(
+            head,
+            my_slopes,
+            bases,
+            queries_t,
+            queries,
+            d_heads_t,
+            d_heads_n,
+            context_t,
+            logsum,
+            keys,
+            keys_t,
+            values,
+            count,
+        )
+        d_head_queries.append(held)
+        d_head_pairs.append(pair)
+    feed = share_rows(lax.psum_scatter(quarter, "fsdp", scatter_dimension=0, tiled=True))
+    out_share = feed[:, :, 3 * hidden_part : 3 * hidden_part + head_width]
+    norm_share = jnp.transpose(feed[:, :, 3 * hidden_part + head_width])
+    d_queries_t = jnp.concatenate(d_head_queries, axis=0)
+
     rows_here = w_gate.shape[0]
 
     def units(shared):
@@ -407,22 +456,30 @@
     def columns(shared):
         return jnp.transpose(shared, (1, 0, 2)).reshape(rows_here, width)
 
-    pending = jnp.transpose(jnp.concatenate((d_keys, d_values), axis=0), (1, 0, 2))
-    pending = pending.reshape(GROUP, seq_rows, 2 * head_width)
-    while pending.shape[0] > 1:
-        half = pending.shape[0] // 2
-        leaving = pending[half:].astype(bf16)
-        pending = pending[:half] + from_partner(leaving, "fsdp", half).astype(f32)
+    summed_pairs = []
+    for pair in d_head_pairs:
+        pending = pair.reshape(GROUP, seq_rows, 2 * HEAD_DIM)
+        while pending.shape[0] > 1:
+            half = pending.shape[0] // 2
+            landed = from_partner(pending[half:], "fsdp", half).astype(f32)
+            pending = (pending[:half].astype(f32) + landed).astype(bf16)
+        summed_pairs.append(pending[0])
+    d_pairs = [pair[:, :HEAD_DIM] for pair in summed_pairs]
+    d_pairs += [pair[:, HEAD_DIM:] for pair in summed_pairs]
     d_queries = jnp.transpose(d_queries_t.reshape(head_width, seq_rows))
-    d_all = jnp.concatenate((d_queries.astype(bf16), pending[0].astype(bf16)), axis=1)
+    d_all = jnp.concatenate([d_queries.astype(bf16)] + d_pairs, axis=1)
     d_all = d_all.reshape(groups, count, 3 * head_width)
     d_rows = [d_all[0]] + [from_sp(d_all[p], p) for p in range(1, groups)]
-    grad_threes = [product_left(source, rows) for rows in d_rows]
+    owner = jnp.arange(owners, dtype=jnp.int32) ^ lax.axis_index("fsdp")
+    swapped = jnp.take(source.reshape(count, owners, rows_here), owner, axis=1, mode="clip")
+    swapped = swapped.reshape(count, width)
+    grad_threes = [product_left(swapped, rows).astype(bf16) for rows in d_rows]
     d_tokens = d_first
     for rows, weight in zip(d_rows, threes):
         d_tokens = d_tokens + product_right(rows, weight)
     input_grad = d_tokens.astype(bf16)[None]
-    three = scatter_rows(sum_to_quarter(grad_threes))
+    three = sum_far(*sum_near(grad_threes)).astype(f32)
+    three = share_rows(halve_rows(three.reshape(owners, rows_here, 3 * head_width)))
     return (
         output,
         input_grad,
@@ -434,7 +491,7 @@
         norm_share[:, 1],
         units(feed[:, :, :hidden_part]),
         units(feed[:, :, hidden_part : 2 * hidden_part]),
-        feed[:, :, 2 * hidden_part :].reshape(groups * piece_part, width),
+        feed[:, :, 2 * hidden_part : 3 * hidden_part].reshape(groups * piece_part, width),
         norm_share[:, 2],
         norm_share[:, 3],
     )

time: 936 us -> 800 us (0.85)
  waiting for transfers between devices: 346 us -> 257 us
  blocking collectives: 101 us -> 42.7 us
  starting transfers between devices: 24.6 us -> 34.6 us
    reduce_scatter x3 -> x1, waiting for transfers between devices: 109 us -> 14.8 us  [body(): lax.psum_scatter(quarter, 'fsdp', scatter_dimension=0, tiled=True)]
    ppermute x41 -> x39, waiting for transfers between devices: 193 us -> 242 us  [from_partner(): lax.ppermute(array, axis, [(i, i ^ distance) for i in range(lax.axis_size...]
    all_gather x2 -> x1, blocking collectives: 82.4 us -> 36.1 us  [gather_rows(): return lax.all_gather(shard, 'fsdp', axis=0, tiled=True)]
    unnamed x9 -> x4, waiting for transfers between devices: 34 us -> 0.07 us
    concatenate x1 -> x5, local copies, waits for them, and re-layouts: 2.39 us -> 26.8 us  [the longest x4 26.8 us: body(): wide.append(jnp.concatenate([part.astype(bf16) for part in parts], axis=1))]
    slice x11 -> x19, local copies, waits for them, and re-layouts: 51.2 us -> 27.7 us  [the longest x8 10.8 us: body(): landed = from_partner(pending[half:], 'fsdp', half).astype(f32)]
    convert_element_type x8 -> x14, other arithmetic: 13.4 us -> 24.6 us  [the longest x1 7.61 us: sum_far(): return (near + from_sp(far, 2).astype(jnp.float32)).astype(jnp.bfloat16)]
    transpose x1 -> x0, other arithmetic: 10.8 us -> none  [body(): jnp.transpose(jnp.concatenate((d_keys, d_values), axis=0), (1, 0, 2))]
  transfers between devices with their start and end apart: 49 -> 43, of which waited for: 19 -> 20; matrix products, arithmetic and copies ran while one was open for 20% -> 19% of each run, Pallas kernels for 18% -> 18%
where the time goes in v2:
time: 800 us; the launch traced here: 792 us
  waiting for transfers between devices  257 us (32%)
  Pallas kernels  177 us (22%)
  local copies, waits for them, and re-layouts  147 us (18%)
  matrix products  65.4 us (8%)
  other arithmetic  52.1 us (7%)
  blocking collectives  42.7 us (5%)
  starting transfers between devices  34.6 us (4%)
  between operations  15.5 us (2%)
    ppermute x39, waiting for transfers between devices, from_partner(): lax.ppermute(array, axis, [(i, i ^ distance) for i in range(lax.axis_size...  242 us
    pallas_call x3, Pallas kernels, attend_backward(): pl.pallas_call(functools.partial(backward_kernel, head, block), grid=(cou...  98.3 us
    pallas_call x1, Pallas kernels, attend_forward(): pl.pallas_call(functools.partial(forward_kernel, block), grid=(heads, cou...  78.5 us
    all_gather x1, blocking collectives, gather_rows(): return lax.all_gather(shard, 'fsdp', axis=0, tiled=True)  36.1 us
    ppermute x39, starting transfers between devices, from_partner(): lax.ppermute(array, axis, [(i, i ^ distance) for i in range(lax.axis_size...  34.3 us
    concatenate x4, local copies, waits for them, and re-layouts, body(): wide.append(jnp.concatenate([part.astype(bf16) for part in parts], axis=1))  26.8 us
    dot_general x11, matrix products, product_left(): lax.dot_general(left, right, (((0,), (0,)), ((), ())), preferred_element_...  23.7 us
    dot_general x8, matrix products, product(): return jnp.dot(left, right, preferred_element_type=jnp.float32)  22.6 us
  transfers between devices with their start and end apart: 43, of which 20 were waited for; matrix products, arithmetic and copies ran while one was open for 19% of the time, Pallas kernels for 18%

profile of v2, /device:TPU:0, one launch (start us, length us, event | category | flops | bytes accessed | tf_op | source)
XLA Modules:
  0.0 791.6 jit_solution(3898173439413807122)
XLA Ops:
  16.3 36.1 %all_gather.21 = bf16[768,576]{1,0:T(8,128)(2,1)S(1)} all-gather(bf16[96,576]{1,0:T(8,128)(2,1)S(1)} %pad_maximum_fusion.20), channel_id=1, replica_groups=mesh['sp'=4,'fsdp'=8] {'fsdp'}, dimensions={0}, use_global_device_ids=true | all-gather | bytes 995328 | tf_op jit(solution)/shard_map/all_gather | solution.py:242
  55.6 15.5 %collective-permute-done.2 = bf16[768,576]{0,1:T(8,128)(2,1)S(1)} collective-permute-done((bf16[768,576]{0,1:T(8,128)(2,1)}, bf16[768,576]{0,1:T(8,128)(2,1)S(1)}, u32[]{:S(2)}, u32[]{:S(2)}) %collective-permute-start.2) | collective-permute-done | bytes 884768 | tf_op jit(solution)/shard_map/ppermute | solution.py:21
  76.2 8.6 %collective-permute-done.3 = bf16[384,576]{0,1:T(8,128)(2,1)S(1)} collective-permute-done((bf16[384,576]{0,1:T(8,128)(2,1)S(1)}, bf16[384,576]{0,1:T(8,128)(2,1)S(1)}, u32[]{:S(2)}, u32[]{:S(2)}) %collective-permute-start.3) | collective-permute-done | bytes 442400 | tf_op jit(solution)/shard_map/ppermute | solution.py:21
  84.8 8.7 %collective-permute-done.5 = bf16[384,576]{0,1:T(8,128)(2,1)S(1)} collective-permute-done((bf16[384,576]{0,1:T(8,128)(2,1)S(1)}, bf16[384,576]{0,1:T(8,128)(2,1)S(1)}, u32[]{:S(2)}, u32[]{:S(2)}) %collective-permute-start.5) | collective-permute-done | bytes 442400 | tf_op jit(solution)/shard_map/ppermute | solution.py:21
  95.8 30.2 %collective-permute-done.6 = bf16[1536,384]{0,1:T(8,128)(2,1)} collective-permute-done((bf16[1536,384]{0,1:T(8,128)(2,1)S(1)}, bf16[1536,384]{0,1:T(8,128)(2,1)}, u32[]{:S(2)}, u32[]{:S(2)}) %collective-permute-start.6) | collective-permute-done | bytes 1179680 | tf_op jit(solution)/shard_map/ppermute | solution.py:21
  135.0 45.0 %collective-permute-done.8 = bf16[1536,384]{0,1:T(8,128)(2,1)} collective-permute-done((bf16[1536,384]{0,1:T(8,128)(2,1)}, bf16[1536,384]{0,1:T(8,128)(2,1)}, u32[]{:S(2)}, u32[]{:S(2)}) %collective-permute-start.8) | collective-permute-done | bytes 1179680 | tf_op jit(solution)/shard_map/ppermute | solution.py:21
  184.6 6.1 copy.221.k_ref
  192.8 78.5 %shard_map.237 = (f32[3,64,1536]{2,1,0:T(8,128)S(1)}, f32[3,1,1536]{2,1,0:T(1,128)S(1)}) custom-call(f32[3]{0:T(128)S(1)} %dynamic_slice.58.slopes_ref, f32[16]{0:T(128)S(1)} %convert_element_type.250.bases_ref, bf16[3,64,1536]{2,1,0:T(8,128)(2,1)S(1)} %bitcast.166, bf16[3,6144,64]{2,1,0:T(8,128)(2,1)} %copy.221.k_ref, ...), custom_call_target="tpu_custom_call" | custom-call | flops 28991029248 | bytes 18874368 | tf_op jit(solution)/shard_map/pallas_call | solution.py:168
  284.7 23.7 %collective-permute-done.16 = bf16[768,768]{1,0:T(8,128)(2,1)} collective-permute-done((bf16[768,768]{1,0:T(8,128)(2,1)}, bf16[768,768]{1,0:T(8,128)(2,1)}, u32[]{:S(2)}, u32[]{:S(2)}) %collective-permute-start.16) | collective-permute-done | bytes 1179680 | tf_op jit(solution)/shard_map/ppermute | solution.py:21
  317.8 11.2 %multiply_convert_fusion.1 = (bf16[384,3072]{1,0:T(8,128)(2,1)S(1)}, f32[384,3072]{1,0:T(8,128)S(1)}, f32[384,3072]{1,0:T(8,128)S(1)}) fusion(f32[384,3072]{1,0:T(8,128)S(1)} %fusion.27, bf16[384,768]{1,0:T(8,128)(2,1)S(1)} %fusion.23, bf16[768,768]{1,0:T(8,128)(2,1)S(1)} %get-tuple-element.101, bf16[768,768]{1,0:T(8,128)(2,1)S(1)} %get-tuple-element.99, ...), kind=kOutput, calls=%fused_computation.16 | convolution fusion | flops 1908670464 | bytes 21823488 | tf_op jit(solution)/shard_map/dot_general | solution.py:40
  340.9 6.6 fusion.24
  407.5 6.9 concatenate.82
  414.4 6.7 concatenate.81
  421.1 6.9 concatenate.80
  428.0 6.2 concatenate.79
  438.1 5.7 copy.241
  444.5 32.6 %shard_map.238 = (f32[1,64,1536]{2,1,0:T(8,128)S(1)}, bf16[6144,128]{1,0:T(8,128)(2,1)}) custom-call(f32[3]{0:T(128)S(1)} %dynamic_slice.58.slopes_ref, f32[16]{0:T(128)S(1)} %convert_element_type.250.bases_ref, bf16[3,64,1536]{2,1,0:T(8,128)(2,1)S(1)} %bitcast.168, bf16[3,1536,64]{2,1,0:T(8,128)(2,1)S(1)} %bitcast.178, bf16[3,64,1536]{2,1,0:T(8,128)(2,1)S(1)} %bitcast.172, ...), custom_call_target="tpu_custom_call" | custom-call | flops 24159191040 | bytes 12582912 | tf_op jit(solution)/shard_map/pallas_call | solution.py:205
  483.1 6.4 add_convert_fusion.1
  489.5 6.5 convert_add_fusion
  497.1 32.6 %shard_map.239 = (f32[1,64,1536]{2,1,0:T(8,128)S(1)}, bf16[6144,128]{1,0:T(8,128)(2,1)}) custom-call(f32[3]{0:T(128)S(1)} %dynamic_slice.58.slopes_ref, f32[16]{0:T(128)S(1)} %convert_element_type.250.bases_ref, bf16[3,64,1536]{2,1,0:T(8,128)(2,1)S(1)} %bitcast.169, bf16[3,1536,64]{2,1,0:T(8,128)(2,1)S(1)} %bitcast.179, bf16[3,64,1536]{2,1,0:T(8,128)(2,1)S(1)} %bitcast.173, ...), custom_call_target="tpu_custom_call" | custom-call | flops 24159191040 | bytes 12582912 | tf_op jit(solution)/shard_map/pallas_call | solution.py:205
  547.4 7.7 collective-permute-done.26
  561.3 5.8 collective-permute-done.27
  568.0 15.4 %collective-permute-done.23 = bf16[768,2560]{1,0:T(8,128)(2,1)} collective-permute-done((bf16[768,2560]{1,0:T(8,128)(2,1)}, bf16[768,2560]{1,0:T(8,128)(2,1)}, u32[]{:S(2)}, u32[]{:S(2)}) %collective-permute-start.23) | collective-permute-done | bytes 3932192 | tf_op jit(solution)/shard_map/ppermute | solution.py:21
  583.4 7.6 add_convert_fusion
  591.7 33.0 %shard_map.240 = (f32[1,64,1536]{2,1,0:T(8,128)S(1)}, bf16[6144,128]{1,0:T(8,128)(2,1)}) custom-call(f32[3]{0:T(128)S(1)} %dynamic_slice.58.slopes_ref, f32[16]{0:T(128)S(1)} %convert_element_type.250.bases_ref, bf16[3,64,1536]{2,1,0:T(8,128)(2,1)S(1)} %bitcast.170, bf16[3,1536,64]{2,1,0:T(8,128)(2,1)S(1)} %bitcast.180, bf16[3,64,1536]{2,1,0:T(8,128)(2,1)S(1)} %bitcast.174, ...), custom_call_target="tpu_custom_call" | custom-call | flops 24159191040 | bytes 12582912 | tf_op jit(solution)/shard_map/pallas_call | solution.py:205
  629.8 33.2 %collective-permute-done.28 = bf16[2,1536,128]{2,1,0:T(8,128)(2,1)S(1)} collective-permute-done((bf16[2,1536,128]{2,1,0:T(8,128)(2,1)S(1)}, bf16[2,1536,128]{2,1,0:T(8,128)(2,1)S(1)}, u32[]{:S(2)}, u32[]{:S(2)}) %collective-permute-start.28) | collective-permute-done | bytes 786464 | tf_op jit(solution)/shard_map/ppermute | solution.py:21
  667.9 6.2 collective-permute-done.29
  680.6 9.0 %collective-permute-done.32 = bf16[384,576]{0,1:T(8,128)(2,1)S(1)} collective-permute-done((bf16[384,576]{0,1:T(8,128)(2,1)}, bf16[384,576]{0,1:T(8,128)(2,1)S(1)}, u32[]{:S(2)}, u32[]{:S(2)}) %collective-permute-start.32) | collective-permute-done | bytes 442400 | tf_op jit(solution)/shard_map/ppermute | solution.py:21
  693.3 9.6 %collective-permute-done.31 = bf16[384,576]{0,1:T(8,128)(2,1)S(1)} collective-permute-done((bf16[384,576]{0,1:T(8,128)(2,1)S(1)}, bf16[384,576]{0,1:T(8,128)(2,1)S(1)}, u32[]{:S(2)}, u32[]{:S(2)}) %collective-permute-start.31) | collective-permute-done | bytes 442400 | tf_op jit(solution)/shard_map/ppermute | solution.py:21
  706.5 14.8 %reduce-scatter.2.cloned.1.call-done = bf16[96,2560]{1,0:T(8,128)(2,1)} async-done(((bf16[768,2560]{1,0:T(8,128)(2,1)}), bf16[96,2560]{1,0:T(8,128)(2,1)}) %reduce-scatter.2.cloned.1.call-update) | async-done | bytes 491536 | tf_op jit(solution)/shard_map/reduce_scatter | solution.py:445
  731.3 8.3 %collective-permute-done.36 = bf16[384,576]{0,1:T(8,128)(2,1)S(1)} collective-permute-done((bf16[384,576]{0,1:T(8,128)(2,1)S(1)}, bf16[384,576]{0,1:T(8,128)(2,1)S(1)}, u32[]{:S(2)}, u32[]{:S(2)}) %collective-permute-start.36) | collective-permute-done | bytes 442400 | tf_op jit(solution)/shard_map/ppermute | solution.py:21
  755.6 6.6 all-gather
  (415 shorter events, 238.1 us)
Async XLA Ops:
  7.2 121.5 %all-gather.8.cloned.1.call-start = ((), (), s32[]{:S(2)}) async-start(), calls=%async_computation.2 | async-start | bytes 2654208 | tf_op jit(solution)/shard_map/all_gather | solution.py:242
  14.1 260.7 %all-gather.6.cloned.1.call-start = ((), (), s32[]{:S(2)}) async-start(), calls=%async_computation.1 | async-start | bytes 2875392 | tf_op jit(solution)/shard_map/all_gather | solution.py:242
  53.7 17.4 %collective-permute-start.2 = (bf16[768,576]{0,1:T(8,128)(2,1)}, bf16[768,576]{0,1:T(8,128)(2,1)S(1)}, u32[]{:S(2)}, u32[]{:S(2)}) collective-permute-start(bf16[768,576]{0,1:T(8,128)(2,1)} %copy.219), channel_id=1, source_target_pairs={{0,16},{8,24},{16,0},{24,8},{1,17},{9,25},{17,1},{25,9},{2,18},{10... | collective-permute-start | bytes 2654216 | tf_op jit(solution)/shard_map/ppermute | solution.py:21
  55.6 17.3 %collective-permute-start = (bf16[768,576]{0,1:T(8,128)(2,1)}, bf16[768,576]{0,1:T(8,128)(2,1)S(1)}, u32[]{:S(2)}, u32[]{:S(2)}) collective-permute-start(bf16[768,576]{0,1:T(8,128)(2,1)} %copy.219), channel_id=1, source_target_pairs={{0,8},{8,0},{16,24},{24,16},{1,9},{9,1},{17,25},{25,17},{2,10},{10... | collective-permute-start | bytes 2654216 | tf_op jit(solution)/shard_map/ppermute | solution.py:21
  71.7 13.0 %collective-permute-start.3 = (bf16[384,576]{0,1:T(8,128)(2,1)S(1)}, bf16[384,576]{0,1:T(8,128)(2,1)S(1)}, u32[]{:S(2)}, u32[]{:S(2)}) collective-permute-start(bf16[384,576]{0,1:T(8,128)(2,1)S(1)} %fusion.17), channel_id=1, source_target_pairs={{0,16},{8,24},{16,0},{24,8},{1,17},{9,25},{17,1},{25,9},{2,18},{10... | collective-permute-start | bytes 1327112 | tf_op jit(solution)/shard_map/ppermute | solution.py:21
  74.5 19.0 %collective-permute-start.5 = (bf16[384,576]{0,1:T(8,128)(2,1)S(1)}, bf16[384,576]{0,1:T(8,128)(2,1)S(1)}, u32[]{:S(2)}, u32[]{:S(2)}) collective-permute-start(bf16[384,576]{0,1:T(8,128)(2,1)S(1)} %fusion.18), channel_id=1, source_target_pairs={{0,24},{8,16},{16,8},{24,0},{1,25},{9,17},{17,9},{25,1},{2,26},{10... | collective-permute-start | bytes 1327112 | tf_op jit(solution)/shard_map/ppermute | solution.py:21
  94.3 31.7 %collective-permute-start.6 = (bf16[1536,384]{0,1:T(8,128)(2,1)S(1)}, bf16[1536,384]{0,1:T(8,128)(2,1)}, u32[]{:S(2)}, u32[]{:S(2)}) collective-permute-start(bf16[1536,384]{0,1:T(8,128)(2,1)S(1)} %pad_maximum_fusion.5), channel_id=1, source_target_pairs={{0,1},{1,0},{2,3},{3,2},{4,5},{5,4},{6,7},{7,6},{8,9},{9,8},{10,11... | collective-permute-start | bytes 3538952 | tf_op jit(solution)/shard_map/ppermute | solution.py:21
  95.4 625.9 %reduce-scatter.2.cloned.1.call-start = ((), (), s32[]{:S(2)}) async-start(), calls=%async_computation.3 | async-start | bytes 4423680 | tf_op jit(solution)/shard_map/reduce_scatter | solution.py:445
  95.7 39.3 %collective-permute-start.7 = (bf16[1536,384]{0,1:T(8,128)(2,1)S(1)}, bf16[1536,384]{0,1:T(8,128)(2,1)}, u32[]{:S(2)}, u32[]{:S(2)}) collective-permute-start(bf16[1536,384]{0,1:T(8,128)(2,1)S(1)} %pad_maximum_fusion.5), channel_id=1, source_target_pairs={{0,2},{1,3},{2,0},{3,1},{4,6},{5,7},{6,4},{7,5},{8,10},{9,11},{10,... | collective-permute-start | bytes 3538952 | tf_op jit(solution)/shard_map/ppermute | solution.py:21
  126.0 54.0 %collective-permute-start.8 = (bf16[1536,384]{0,1:T(8,128)(2,1)}, bf16[1536,384]{0,1:T(8,128)(2,1)}, u32[]{:S(2)}, u32[]{:S(2)}) collective-permute-start(bf16[1536,384]{0,1:T(8,128)(2,1)} %collective-permute-done.6), channel_id=1, source_target_pairs={{0,2},{1,3},{2,0},{3,1},{4,6},{5,7},{6,4},{7,5},{8,10},{9,11},{10,... | collective-permute-start | bytes 3538952 | tf_op jit(solution)/shard_map/ppermute | solution.py:21
  128.8 142.9 %collective-permute-start.13 = (bf16[768,1536]{1,0:T(8,128)(2,1)}, bf16[768,1536]{1,0:T(8,128)(2,1)}, u32[]{:S(2)}, u32[]{:S(2)}) collective-permute-start(bf16[768,1536]{1,0:T(8,128)(2,1)} %all-gather.8.cloned.1.call-done), channel_id=1, source_target_pairs={{0,16},{8,24},{16,0},{24,8},{1,17},{9,25},{17,1},{25,9},{2,18},{10... | collective-permute-start | bytes 7077896 | tf_op jit(solution)/shard_map/ppermute | solution.py:21
  129.9 180.3 %collective-permute-start.12 = (bf16[768,1536]{1,0:T(8,128)(2,1)}, bf16[768,1536]{1,0:T(8,128)(2,1)}, u32[]{:S(2)}, u32[]{:S(2)}) collective-permute-start(bf16[768,1536]{1,0:T(8,128)(2,1)} %all-gather.8.cloned.1.call-done), channel_id=1, source_target_pairs={{0,8},{8,0},{16,24},{24,16},{1,9},{9,1},{17,25},{25,17},{2,10},{10... | collective-permute-start | bytes 7077896 | tf_op jit(solution)/shard_map/ppermute | solution.py:21
  271.6 41.2 %collective-permute-start.14 = (bf16[768,1536]{1,0:T(8,128)(2,1)}, bf16[768,1536]{1,0:T(8,128)(2,1)}, u32[]{:S(2)}, u32[]{:S(2)}) collective-permute-start(bf16[768,1536]{1,0:T(8,128)(2,1)} %collective-permute-done.13), channel_id=1, source_target_pairs={{0,8},{8,0},{16,24},{24,16},{1,9},{9,1},{17,25},{25,17},{2,10},{10... | collective-permute-start | bytes 7077896 | tf_op jit(solution)/shard_map/ppermute | solution.py:21
  279.4 29.0 %collective-permute-start.16 = (bf16[768,768]{1,0:T(8,128)(2,1)}, bf16[768,768]{1,0:T(8,128)(2,1)}, u32[]{:S(2)}, u32[]{:S(2)}) collective-permute-start(bf16[768,768]{1,0:T(8,128)(2,1)} %slice.403), channel_id=1, source_target_pairs={{0,16},{8,24},{16,0},{24,8},{1,17},{9,25},{17,1},{25,9},{2,18},{10... | collective-permute-start | bytes 3538952 | tf_op jit(solution)/shard_map/ppermute | solution.py:21
  280.5 48.5 %collective-permute-start.15 = (bf16[768,768]{1,0:T(8,128)(2,1)}, bf16[768,768]{1,0:T(8,128)(2,1)}, u32[]{:S(2)}, u32[]{:S(2)}) collective-permute-start(bf16[768,768]{1,0:T(8,128)(2,1)} %slice.403), channel_id=1, source_target_pairs={{0,8},{8,0},{16,24},{24,16},{1,9},{9,1},{17,25},{25,17},{2,10},{10... | collective-permute-start | bytes 3538952 | tf_op jit(solution)/shard_map/ppermute | solution.py:21
  308.4 20.6 %collective-permute-start.17 = (bf16[768,768]{1,0:T(8,128)(2,1)}, bf16[768,768]{1,0:T(8,128)(2,1)S(1)}, u32[]{:S(2)}, u32[]{:S(2)}) collective-permute-start(bf16[768,768]{1,0:T(8,128)(2,1)} %collective-permute-done.16), channel_id=1, source_target_pairs={{0,8},{8,0},{16,24},{24,16},{1,9},{9,1},{17,25},{25,17},{2,10},{10... | collective-permute-start | bytes 3538952 | tf_op jit(solution)/shard_map/ppermute | solution.py:21
  401.6 32.7 %collective-permute-start.18 = (bf16[384,192]{1,0:T(8,128)(2,1)}, bf16[384,192]{1,0:T(8,128)(2,1)}, u32[]{:S(2)}, u32[]{:S(2)}) collective-permute-start(bf16[384,192]{1,0:T(8,128)(2,1)} %get-tuple-element.125), channel_id=1, source_target_pairs={{0,8},{8,0},{16,24},{24,16},{1,9},{9,1},{17,25},{25,17},{2,10},{10... | collective-permute-start | bytes 442376 | tf_op jit(solution)/shard_map/ppermute | solution.py:21
  402.0 32.2 %collective-permute-start.19 = (bf16[384,192]{1,0:T(8,128)(2,1)}, bf16[384,192]{1,0:T(8,128)(2,1)}, u32[]{:S(2)}, u32[]{:S(2)}) collective-permute-start(bf16[384,192]{1,0:T(8,128)(2,1)} %get-tuple-element.124), channel_id=1, source_target_pairs={{0,16},{8,24},{16,0},{24,8},{1,17},{9,25},{17,1},{25,9},{2,18},{10... | collective-permute-start | bytes 442376 | tf_op jit(solution)/shard_map/ppermute | solution.py:21
  403.1 31.1 %collective-permute-start.20 = (bf16[384,192]{1,0:T(8,128)(2,1)}, bf16[384,192]{1,0:T(8,128)(2,1)}, u32[]{:S(2)}, u32[]{:S(2)}) collective-permute-start(bf16[384,192]{1,0:T(8,128)(2,1)} %get-tuple-element.123), channel_id=1, source_target_pairs={{0,24},{8,16},{16,8},{24,0},{1,25},{9,17},{17,9},{25,1},{2,26},{10... | collective-permute-start | bytes 442376 | tf_op jit(solution)/shard_map/ppermute | solution.py:21
  436.5 46.6 %collective-permute-start.22 = (bf16[768,2560]{1,0:T(8,128)(2,1)}, bf16[768,2560]{1,0:T(8,128)(2,1)}, u32[]{:S(2)}, u32[]{:S(2)}) collective-permute-start(bf16[768,2560]{1,0:T(8,128)(2,1)} %concatenate.82), channel_id=1, source_target_pairs={{0,8},{8,0},{16,24},{24,16},{1,9},{9,1},{17,25},{25,17},{2,10},{10... | collective-permute-start | bytes 11796488 | tf_op jit(solution)/shard_map/ppermute | solution.py:21
  443.8 45.8 %collective-permute-start.21 = (bf16[768,2560]{1,0:T(8,128)(2,1)}, bf16[768,2560]{1,0:T(8,128)(2,1)}, u32[]{:S(2)}, u32[]{:S(2)}) collective-permute-start(bf16[768,2560]{1,0:T(8,128)(2,1)} %concatenate.80), channel_id=1, source_target_pairs={{0,8},{8,0},{16,24},{24,16},{1,9},{9,1},{17,25},{25,17},{2,10},{10... | collective-permute-start | bytes 11796488 | tf_op jit(solution)/shard_map/ppermute | solution.py:21
  482.8 56.9 %collective-permute-start.24 = (bf16[2,1536,128]{1,2,0:T(8,128)(2,1)}, bf16[2,1536,128]{1,2,0:T(8,128)(2,1)}, u32[]{:S(2)}, u32[]{:S(2)}) collective-permute-start(bf16[2,1536,128]{1,2,0:T(8,128)(2,1)} %copy.245), channel_id=1, source_target_pairs={{0,2},{1,3},{2,0},{3,1},{4,6},{5,7},{6,4},{7,5},{8,10},{9,11},{10,... | collective-permute-start | bytes 2359304 | tf_op jit(solution)/shard_map/ppermute | solution.py:21
  496.0 87.4 %collective-permute-start.23 = (bf16[768,2560]{1,0:T(8,128)(2,1)}, bf16[768,2560]{1,0:T(8,128)(2,1)}, u32[]{:S(2)}, u32[]{:S(2)}) collective-permute-start(bf16[768,2560]{1,0:T(8,128)(2,1)} %add_convert_fusion.1), channel_id=1, source_target_pairs={{0,16},{8,24},{16,0},{24,8},{1,17},{9,25},{17,1},{25,9},{2,18},{10... | collective-permute-start | bytes 11796488 | tf_op jit(solution)/shard_map/ppermute | solution.py:21
  535.4 19.7 %collective-permute-start.26 = (bf16[2,1536,128]{1,2,0:T(8,128)(2,1)}, bf16[2,1536,128]{1,2,0:T(8,128)(2,1)}, u32[]{:S(2)}, u32[]{:S(2)}) collective-permute-start(bf16[2,1536,128]{1,2,0:T(8,128)(2,1)} %copy.247), channel_id=1, source_target_pairs={{0,2},{1,3},{2,0},{3,1},{4,6},{5,7},{6,4},{7,5},{8,10},{9,11},{10,... | collective-permute-start | bytes 2359304 | tf_op jit(solution)/shard_map/ppermute | solution.py:21
  543.2 15.6 %collective-permute-start.25 = (bf16[1,1536,128]{1,2,0:T(8,128)(2,1)}, bf16[1,1536,128]{1,2,0:T(8,128)(2,1)}, u32[]{:S(2)}, u32[]{:S(2)}) collective-permute-start(bf16[1,1536,128]{1,2,0:T(8,128)(2,1)} %slice.419), channel_id=1, source_target_pairs={{0,1},{1,0},{2,3},{3,2},{4,5},{5,4},{6,7},{7,6},{8,9},{9,8},{10,11... | collective-permute-start | bytes 1179656 | tf_op jit(solution)/shard_map/ppermute | solution.py:21
  625.5 140.6 %all-gather.10.cloned.1.call-start = ((), (), s32[]{:S(2)}) async-start(), calls=%async_computation.4 | async-start | bytes 2457600 | tf_op jit(solution)/shard_map/all_gather | solution.py:277
  627.0 36.1 %collective-permute-start.28 = (bf16[2,1536,128]{2,1,0:T(8,128)(2,1)S(1)}, bf16[2,1536,128]{2,1,0:T(8,128)(2,1)S(1)}, u32[]{:S(2)}, u32[]{:S(2)}) collective-permute-start(bf16[2,1536,128]{2,1,0:T(8,128)(2,1)S(1)} %bitcast.215), channel_id=1, source_target_pairs={{0,2},{1,3},{2,0},{3,1},{4,6},{5,7},{6,4},{7,5},{8,10},{9,11},{10,... | collective-permute-start | bytes 2359304 | tf_op jit(solution)/shard_map/ppermute | solution.py:21
  677.5 12.1 %collective-permute-start.32 = (bf16[384,576]{0,1:T(8,128)(2,1)}, bf16[384,576]{0,1:T(8,128)(2,1)S(1)}, u32[]{:S(2)}, u32[]{:S(2)}) collective-permute-start(bf16[384,576]{0,1:T(8,128)(2,1)} %get-tuple-element.105), channel_id=1, source_target_pairs={{0,24},{8,16},{16,8},{24,0},{1,25},{9,17},{17,9},{25,1},{2,26},{10... | collective-permute-start | bytes 1327112 | tf_op jit(solution)/shard_map/ppermute | solution.py:21
  690.2 13.3 %collective-permute-start.34 = (bf16[768,576]{0,1:T(8,128)(2,1)S(1)}, bf16[768,576]{0,1:T(8,128)(2,1)S(1)}, u32[]{:S(2)}, u32[]{:S(2)}) collective-permute-start(bf16[768,576]{0,1:T(8,128)(2,1)S(1)} %convolution_convert_fusion.3), channel_id=1, source_target_pairs={{0,8},{8,0},{16,24},{24,16},{1,9},{9,1},{17,25},{25,17},{2,10},{10... | collective-permute-start | bytes 2654216 | tf_op jit(solution)/shard_map/ppermute | solution.py:21
  690.3 12.6 %collective-permute-start.31 = (bf16[384,576]{0,1:T(8,128)(2,1)S(1)}, bf16[384,576]{0,1:T(8,128)(2,1)S(1)}, u32[]{:S(2)}, u32[]{:S(2)}) collective-permute-start(bf16[384,576]{0,1:T(8,128)(2,1)S(1)} %copy-done.65), channel_id=1, source_target_pairs={{0,16},{8,24},{16,0},{24,8},{1,17},{9,25},{17,1},{25,9},{2,18},{10... | collective-permute-start | bytes 1327112 | tf_op jit(solution)/shard_map/ppermute | solution.py:21
  693.1 28.2 %collective-permute-start.33 = (bf16[768,576]{0,1:T(8,128)(2,1)}, bf16[768,576]{0,1:T(8,128)(2,1)}, u32[]{:S(2)}, u32[]{:S(2)}) collective-permute-start(bf16[768,576]{0,1:T(8,128)(2,1)} %convolution_convert_fusion.5), channel_id=1, source_target_pairs={{0,8},{8,0},{16,24},{24,16},{1,9},{9,1},{17,25},{25,17},{2,10},{10... | collective-permute-start | bytes 2654216 | tf_op jit(solution)/shard_map/ppermute | solution.py:21
  704.7 21.5 %collective-permute-start.35 = (bf16[768,576]{0,1:T(8,128)(2,1)}, bf16[768,576]{0,1:T(8,128)(2,1)}, u32[]{:S(2)}, u32[]{:S(2)}) collective-permute-start(bf16[768,576]{0,1:T(8,128)(2,1)} %add_convert_fusion.4), channel_id=1, source_target_pairs={{0,16},{8,24},{16,0},{24,8},{1,17},{9,25},{17,1},{25,9},{2,18},{10... | collective-permute-start | bytes 2654216 | tf_op jit(solution)/shard_map/ppermute | solution.py:21
  (91 other events, 773.3 us)
Sparse Core Ops, SparseCore 0:
  14.2 59.9 all-gather.7
  95.5 78.2 all-gather.5
  625.6 95.6 reduce-scatter.1
  722.8 21.5 all-gather.9
